TPU v7x, 512 devices: a whole 4x4x16 slice. The times are simulated.
512 devices in a mesh: req: 8 (over x, core), head: 4 (over y), ctx: 16 (over z).
Axes of the slice: x: 4, y: 4, z: 16, core: 2. Of those that a mesh axis runs over, the one named last changes fastest.
Arguments:
- xz: bfloat16 [128, 2, 16384], P('req', None, ('head', 'ctx')), may hold values from -6 to 6
- conv_state: bfloat16 [128, 3, 16384], P('req', None, ('head', 'ctx')), may hold values from -6 to 6
- ssm_state: float32 [128, 16, 16384], P('req', None, ('head', 'ctx')), may hold values from -6 to 6
- conv_weight: float32 [4, 16384], P(None, ('head', 'ctx')), may hold values from -3 to 3
- conv_bias: float32 [16384], P(('head', 'ctx')), may hold values from -3 to 3
- x_proj: bfloat16 [16384, 544], P(('head', 'ctx')), may hold values from -0.046875 to 0.046875
- dt_norm_gain: float32 [512], replicated, may hold values from 0.1 to 1.9
- dt_proj: bfloat16 [512, 16384], P(None, ('head', 'ctx')), may hold values from -0.25 to 0.25
- dt_bias: float32 [16384], P(('head', 'ctx')), may hold values from -2 to 1
- a_log: float32 [16, 16384], P(None, ('head', 'ctx')), may hold values from -3 to 2.5
- d_skip: float32 [16384], P(('head', 'ctx')), may hold values from 0.5 to 1.5
- query: bfloat16 [128, 8192], P(('req', 'ctx'), 'head'), may hold values from -16 to 16
- new_kv: bfloat16 [128, 2048], P(('req', 'ctx'), 'head'), may hold values from -6 to 6
- kv_pool: bfloat16 [2560, 64, 2048], P(('req', 'ctx'), None, 'head'), may hold values from -4 to 4
- page_sel: int32 [128, 16], P(('req', 'ctx')), may hold values from 0 to 319, as said below
- lengths: int32 [128], P(('req', 'ctx')), may hold values from 1 to 64
Outputs:
- mamba_out: bfloat16 [128, 16384], P('req', ('head', 'ctx'))
- new_state: float32 [128, 16, 16384], P('req', None, ('head', 'ctx'))
- attention_out: bfloat16 [128, 8192], P(('req', 'ctx'), 'head')
Inputs may be any that keep to these rules, and one draw needn't show every extreme that they name: `page_sel`: entry c * 20 + s names slot s of the pool of context shard c in the request's group (the 16 requests on one index of req). A request's pages are distinct, no page belongs to two requests, and the first entry is the request's newest page. Each request has exactly 3 of its pages on 4 context shards, one page on 4 others and none on the rest; every context shard holds exactly 16 selected pages of its group.
All inputs are finite; a program needn't handle non-finite values.
Results may differ from a plain program's by a relative error of at most 0.017.
Values may be sent and summed in bfloat16 or wider, within the bound.
A program may use at most 64 MiB of HBM per device.

v0:
```python
import math

import jax
import jax.numpy as jnp
from jax import lax
from jax.sharding import PartitionSpec as P

STATE = 16
DT_RANK = 512
Q_HEADS = 64
KV_HEADS = 8
HEAD_DIM = 128
PAGE = 64
MOST = 3


epsilon = 1e-06
far_below = -1e30


def finish_mamba(
    projected, mixed_bf, gating, ssm_state, dt_norm_gain, dt_proj, dt_bias, a_log, d_skip
):
    dt_low = projected[:, :DT_RANK]
    b_terms = projected[:, DT_RANK : DT_RANK + STATE]
    c_terms = projected[:, DT_RANK + STATE : DT_RANK + 2 * STATE]
    inv_rms = lax.rsqrt(jnp.mean(dt_low * dt_low, axis=1, keepdims=True) + epsilon)
    normed = (dt_low * inv_rms * dt_norm_gain[None, :]).astype(jnp.bfloat16)
    step_size = jax.nn.softplus(
        jnp.dot(normed, dt_proj, preferred_element_type=jnp.float32) + dt_bias[None, :]
    )
    mixed_f = mixed_bf.astype(jnp.float32)
    decay_rate = jnp.exp(step_size[:, None, :] * (-jnp.exp(a_log))[None, :, :])
    new_state = decay_rate * ssm_state + (step_size * mixed_f)[:, None, :] * b_terms[:, :, None]
    readout = jnp.sum(c_terms[:, :, None] * new_state, axis=1) + d_skip[None, :] * mixed_f
    mamba_out = (readout * jax.nn.silu(gating)).astype(jnp.bfloat16)
    return (mamba_out, new_state)


def slot_tables(listed, my_shard, pool_size):
    on_shard = (listed // pool_size == my_shard).astype(jnp.int32)
    order_rank = jnp.cumsum(on_shard, axis=-1) - on_shard
    slot_ids = jnp.arange(MOST, dtype=jnp.int32)
    chosen = on_shard[..., None, :] * (order_rank[..., None, :] == slot_ids[:, None]).astype(
        jnp.int32
    )
    slot_index = jnp.sum(chosen * (listed % pool_size)[..., None, :], axis=-1)
    slot_used = jnp.sum(chosen, axis=-1) > 0
    slot_first = chosen[..., 0] > 0
    return (slot_index, slot_used, slot_first)


def token_mask(slot_used, slot_first, length):
    tokens = jnp.arange(PAGE, dtype=jnp.int32)
    return slot_used[..., None] & (
        jnp.logical_not(slot_first)[..., None] | (tokens < length[..., None])
    )


def combine(own_score, fresh_value, part_sum, part_top, part_total):
    row_top = jnp.maximum(jnp.max(part_top, axis=0), own_score)
    factor = jnp.exp(part_top - row_top[None])
    own_weight = jnp.exp(own_score - row_top)
    row_total = jnp.sum(part_total * factor, axis=0) + own_weight
    summed = (
        jnp.sum(part_sum * factor[..., None], axis=0)
        + own_weight[..., None] * fresh_value[:, :, None, :]
    )
    return summed / row_total[..., None]


def on_device(
    xz,
    conv_state,
    ssm_state,
    conv_weight,
    conv_bias,
    x_proj,
    dt_norm_gain,
    dt_proj,
    dt_bias,
    a_log,
    d_skip,
    query,
    new_kv,
    kv_pool,
    page_sel,
    lengths,
):
    inputs = xz[:, 0, :].astype(jnp.float32)
    gating = xz[:, 1, :].astype(jnp.float32)
    window = jnp.concatenate([conv_state.astype(jnp.float32), inputs[:, None, :]], axis=1)
    convolved = jnp.sum(window * conv_weight[None, :, :], axis=1) + conv_bias[None, :]
    mixed_bf = jax.nn.silu(convolved).astype(jnp.bfloat16)
    projected = lax.psum(
        jnp.dot(mixed_bf, x_proj, preferred_element_type=jnp.float32), ("head", "ctx")
    )
    mamba_out, new_state = finish_mamba(
        projected, mixed_bf, gating, ssm_state, dt_norm_gain, dt_proj, dt_bias, a_log, d_skip
    )
    ctx_count = lax.axis_size("ctx")
    my_shard = lax.axis_index("ctx")
    pool_size = kv_pool.shape[0]
    local_rows = query.shape[0]
    kv_local = kv_pool.shape[2] // (2 * HEAD_DIM)
    per_group = Q_HEADS // KV_HEADS
    score_scale = 1.0 / math.sqrt(HEAD_DIM)
    query_heads = query.reshape(local_rows, kv_local, per_group, HEAD_DIM)
    fresh_kv = new_kv.reshape(local_rows, kv_local, 2, HEAD_DIM)
    own_score = (
        jnp.einsum(
            "thd,thgd->thg", fresh_kv[:, :, 0, :], query_heads, preferred_element_type=jnp.float32
        )
        * score_scale
    )
    listed = lax.all_gather(page_sel, "ctx", axis=0, tiled=True)
    slot_index, slot_used, slot_first = slot_tables(listed, my_shard, pool_size)
    outgoing = jnp.take(kv_pool, slot_index, axis=0)
    incoming = lax.all_to_all(outgoing, "ctx", split_axis=0, concat_axis=0, tiled=True)
    incoming = incoming.reshape(ctx_count, local_rows, MOST, PAGE, kv_local, 2, HEAD_DIM)
    shard_ids = jnp.arange(ctx_count, dtype=jnp.int32)[None, :, None]
    owned_index, owned_used, owned_first = slot_tables(page_sel[:, None, :], shard_ids, pool_size)
    usable = token_mask(owned_used, owned_first, lengths[:, None, None])
    scores = (
        jnp.einsum(
            "atmphd,thgd->thgamp",
            incoming[..., 0, :],
            query_heads,
            preferred_element_type=jnp.float32,
        )
        * score_scale
    )
    masked = jnp.where(usable[:, None, None], scores, far_below)
    row_top = jnp.max(masked, axis=(3, 4, 5))
    weights = jnp.where(
        usable[:, None, None], jnp.exp(masked - row_top[..., None, None, None]), 0.0
    )
    row_total = jnp.sum(weights, axis=(3, 4, 5))
    summed = jnp.einsum(
        "thgamp,atmphd->thgd",
        weights,
        incoming[..., 1, :].astype(jnp.float32),
        precision=lax.Precision.HIGHEST,
    )
    part_sum = summed[None]
    part_top = row_top[None]
    part_total = row_total[None]
    attention = combine(
        own_score, fresh_kv[:, :, 1, :].astype(jnp.float32), part_sum, part_top, part_total
    )
    attention_out = attention.reshape(local_rows, kv_local * per_group * HEAD_DIM).astype(
        jnp.bfloat16
    )
    return (mamba_out, new_state, attention_out)


def solution(mesh):
    placed = (
        P("req", None, ("head", "ctx")),
        P("req", None, ("head", "ctx")),
        P("req", None, ("head", "ctx")),
        P(None, ("head", "ctx")),
        P(("head", "ctx")),
        P(("head", "ctx"), None),
        P(),
        P(None, ("head", "ctx")),
        P(("head", "ctx")),
        P(None, ("head", "ctx")),
        P(("head", "ctx")),
        P(("req", "ctx"), "head"),
        P(("req", "ctx"), "head"),
        P(("req", "ctx"), None, "head"),
        P(("req", "ctx"), None),
        P(("req", "ctx")),
    )
    return jax.shard_map(
        on_device,
        mesh=mesh,
        in_specs=placed,
        out_specs=(
            P("req", ("head", "ctx")),
            P("req", None, ("head", "ctx")),
            P(("req", "ctx"), "head"),
        ),
        check_vma=False,
    )
```

profile of v0, /device:TPU:6, one launch (start us, length us, event | category | flops | bytes accessed | tf_op | source)
XLA Modules:
  0.0 468.5 jit_solution(9564047070274278602)
XLA Ops:
  0.6 0.0 copy-start
  0.6 35.5 %all-gather = s32[16,1,16]{2,1,0:T(1,128)S(1)} all-gather(s32[1,1,16]{2,1,0:T(1,128)} %bitcast.123), channel_id=1, replica_groups=mesh['req'=8,'head'=4,'ctx'=16] {'ctx'}, dimensions={0}, use_global_device_ids=true | all-gather | bytes 1088 | tf_op jit(solution)/shard_map/all_gather | solution.py:116
  36.2 0.2 reduce_window_sum.23
  36.4 0.1 multiply_reduce_fusion.3
  36.5 0.1 copy.68
  36.6 0.1 reshape.381
  36.7 0.1 copy.67
  36.8 0.0 copy-done
  36.8 2.5 gather_fusion
  39.4 3.9 broadcast_select_fusion
  43.3 0.0 copy-start.5
  43.3 0.0 copy-start.9
  43.3 0.0 copy-start.1
  43.3 0.0 copy-start.7
  43.3 0.0 copy-start.6
  43.4 0.0 copy-start.3
  43.4 0.0 copy-start.10
  43.4 0.0 copy-start.12
  43.4 0.0 copy-start.2
  43.4 0.0 copy-start.13
  43.4 6.9 %all-to-all-start = ((bf16[16,3,64,512]{3,2,1,0:T(8,128)(2,1)}), bf16[16,3,64,512]{3,2,1,0:T(8,128)(2,1)}, u32[]{:S(2)}, u32[]{:S(2)}) async-start(bf16[16,3,64,512]{3,2,1,0:T(8,128)(2,1)} %broadcast_select_fusion), calls=%async_computation | async-start | bytes 6291456 | tf_op jit(solution)/shard_map/all_to_all | solution.py:119
  50.3 0.0 copy-done.14
  50.4 0.2 reduce_window_sum.22
  50.5 0.1 copy.61
  50.6 0.1 copy.60
  50.7 0.1 copy.62
  50.8 0.1 copy.63
  51.6 0.0 copy-done.8
  51.6 0.0 copy-done.11
  51.7 0.0 copy-done.4
  51.8 0.0 copy-done.5
  51.8 0.2 fusion.37
  52.0 397.6 %psum.7 = f32[16,544]{1,0:T(8,128)S(1)} all-reduce(f32[16,544]{1,0:T(8,128)S(1)} %fusion.37), channel_id=1, replica_groups=mesh['req'=8,'head'=4,'ctx'=16] {'head','ctx'}, use_global_device_ids=true, to_apply=%region_1.2 | all-reduce | flops 8704 | bytes 69632 | tf_op jit(solution)/shard_map/psum | solution.py:95
  449.6 0.1 multiply_reduce_fusion.2
  449.7 0.1 fusion.26
  449.8 0.1 or_and_fusion
  450.0 0.1 fusion.42
  450.1 0.2 convert_multiply_fusion.2
  450.3 0.0 copy-done.2
  450.3 0.8 multiply_reduce_fusion
  451.1 0.6 fusion.14
  451.8 0.0 all-to-all-done
  451.8 5.5 %reshape.371 = bf16[16,1,3,64,2,2,128]{6,5,4,3,2,0,1:T(2,128)(2,1)} reshape(bf16[16,3,64,512]{3,2,1,0:T(8,128)(2,1)} %all-to-all-done) | data formatting | bytes 6291456 | tf_op jit(solution)/shard_map/reshape | solution.py:120
  457.3 8.1 %fusion.41 = (bf16[16,1,3,64,2,1,128]{6,5,4,3,2,0,1:T(2,128)(2,1)S(1)}, bf16[16,1,3,64,2,1,128]{6,5,4,3,2,0,1:T(2,128)(2,1)S(1)}) fusion(bf16[16,1,3,64,2,2,128]{6,5,4,3,2,0,1:T(2,128)(2,1)} %reshape.371), kind=kLoop, calls=%fused_computation.82 | loop fusion | bytes 6291456 | tf_op jit(solution)/shard_map/slice | solution.py:127
  465.3 1.4 fusion.45
  466.8 0.3 fusion.40
  467.0 0.8 fusion.9
  467.9 0.6 convert_element_type.73
  (36 shorter events, 0.3 us)
Async XLA Ops:
  0.6 36.2 %copy-start = (bf16[20,64,512]{2,1,0:T(8,128)(2,1)S(1)}, bf16[20,64,512]{2,1,0:T(8,128)(2,1)}, u32[]{:S(2)}) copy-start(bf16[20,64,512]{2,1,0:T(8,128)(2,1)} %param.29) | copy-start | bytes 3932164
  43.3 7.1 %copy-start.14 = (s32[1,16]{1,0:T(1,128)S(1)}, s32[1,16]{1,0:T(1,128)}, u32[]{:S(2)}) copy-start(s32[1,16]{1,0:T(1,128)} %param.30) | copy-start | bytes 196
  43.3 8.3 %copy-start.8 = (bf16[1,2048]{1,0:T(2,128)(2,1)S(1)}, bf16[1,2048]{1,0:T(2,128)(2,1)}, u32[]{:S(2)}) copy-start(bf16[1,2048]{1,0:T(2,128)(2,1)} %param.27) | copy-start | bytes 12292
  43.3 8.4 %copy-start.11 = (bf16[1,512]{1,0:T(2,128)(2,1)S(1)}, bf16[1,512]{1,0:T(2,128)(2,1)}, u32[]{:S(2)}) copy-start(bf16[1,512]{1,0:T(2,128)(2,1)} %param.28) | copy-start | bytes 3076
  43.3 8.4 %copy-start.4 = (bf16[16,2,256]{2,1,0:T(2,128)(2,1)S(1)}, bf16[16,2,256]{2,1,0:T(2,128)(2,1)}, u32[]{:S(2)}) copy-start(bf16[16,2,256]{2,1,0:T(2,128)(2,1)} %param.16) | copy-start | bytes 49156
  43.3 8.5 %copy-start.5 = (bf16[16,3,256]{2,0,1:T(8,128)(2,1)S(1)}, bf16[16,3,256]{2,0,1:T(8,128)(2,1)}, u32[]{:S(2)}) copy-start(bf16[16,3,256]{2,0,1:T(8,128)(2,1)} %param.17) | copy-start | bytes 73732
  43.3 8.5 %copy-start.9 = (f32[4,256]{1,0:T(4,128)S(1)}, f32[4,256]{1,0:T(4,128)}, u32[]{:S(2)}) copy-start(f32[4,256]{1,0:T(4,128)} %param.19) | copy-start | bytes 12292
  43.3 8.5 %copy-start.1 = (bf16[256,544]{0,1:T(8,128)(2,1)S(1)}, bf16[256,544]{0,1:T(8,128)(2,1)}, u32[]{:S(2)}) copy-start(bf16[256,544]{0,1:T(8,128)(2,1)} %param.21) | copy-start | bytes 835588
  43.3 8.5 %copy-start.7 = (f32[256]{0:T(256)S(1)}, f32[256]{0:T(256)}, u32[]{:S(2)}) copy-start(f32[256]{0:T(256)} %param.20) | copy-start | bytes 3076
  43.3 406.7 %copy-start.6 = (f32[16,256]{1,0:T(8,128)S(1)}, f32[16,256]{1,0:T(8,128)}, u32[]{:S(2)}) copy-start(f32[16,256]{1,0:T(8,128)} %param.25) | copy-start | bytes 49156
  43.4 406.7 %copy-start.3 = (bf16[512,256]{1,0:T(8,128)(2,1)S(1)}, bf16[512,256]{1,0:T(8,128)(2,1)}, u32[]{:S(2)}) copy-start(bf16[512,256]{1,0:T(8,128)(2,1)} %param.23) | copy-start | bytes 786436
  43.4 406.7 %copy-start.10 = (f32[512]{0:T(512)S(1)}, f32[512]{0:T(512)}, u32[]{:S(2)}) copy-start(f32[512]{0:T(512)} %param.22) | copy-start | bytes 6148
  43.4 406.7 %copy-start.12 = (f32[256]{0:T(256)S(1)}, f32[256]{0:T(256)}, u32[]{:S(2)}) copy-start(f32[256]{0:T(256)} %param.24) | copy-start | bytes 3076
  43.4 406.9 %copy-start.2 = (f32[16,16,256]{2,1,0:T(8,128)S(1)}, f32[16,16,256]{2,1,0:T(8,128)}, u32[]{:S(2)}) copy-start(f32[16,16,256]{2,1,0:T(8,128)} %param.18) | copy-start | bytes 786436
  43.4 407.7 %copy-start.13 = (f32[256]{0:T(256)S(1)}, f32[256]{0:T(256)}, u32[]{:S(2)}) copy-start(f32[256]{0:T(256)} %param.26) | copy-start | bytes 3076
  43.4 408.3 %all-to-all-start = ((bf16[16,3,64,512]{3,2,1,0:T(8,128)(2,1)}), bf16[16,3,64,512]{3,2,1,0:T(8,128)(2,1)}, u32[]{:S(2)}, u32[]{:S(2)}) async-start(bf16[16,3,64,512]{3,2,1,0:T(8,128)(2,1)} %broadcast_select_fusion), calls=%async_computation | async-start | bytes 6291456 | tf_op jit(solution)/shard_map/all_to_all | solution.py:119
where the time goes:
time: 469 us
  blocking collectives  433 us (92%)
  local copies, waits for them, and re-layouts  17.5 us (4%)
  starting transfers between devices  6.91 us (1%)
  other arithmetic  6.59 us (1%)
    psum x1, blocking collectives, on_device(): lax.psum(jnp.dot(mixed_bf, x_proj, preferred_element_type=jnp.float32), (...  398 us
    all_gather x1, blocking collectives, on_device(): listed = lax.all_gather(page_sel, 'ctx', axis=0, tiled=True)  35.5 us
  transfers between devices with their start and end apart: 1, of which 0 were waited for; matrix products, arithmetic and copies ran while one was open for 1% of the time, Pallas kernels for 0%

commit v1 on v0

v1 whole, which is shorter than its diff:
```python
import functools
import math

import jax
import jax.numpy as jnp
from jax import lax
from jax.experimental import pallas as pl
from jax.experimental.pallas import tpu as pltpu
from jax.sharding import PartitionSpec as P

MESH = pl.DeviceIdType.MESH
STATE = 16
DT_RANK = 512
Q_HEADS = 64
KV_HEADS = 8
HEAD_DIM = 128
PAGE = 64
NZ = 16
NY = 4
POOL = 20
TOPK = 16
EPS = 1e-06
FAR_BELOW = -1e30
FLOOR = -1e29
F32 = jnp.float32
BF16 = jnp.bfloat16

Z_ORDER = (8, 7, 9, 6, 10, 5, 11, 4, 12, 3, 13, 2, 14, 1, 15)
SCALE2 = math.log2(math.e) / math.sqrt(HEAD_DIM)


def silu(v):
    return v / (1.0 + jnp.exp(-v))


def split3(v):
    hi = v.astype(BF16).astype(F32)
    rest = v - hi
    mid = rest.astype(BF16).astype(F32)
    return hi, mid, rest - mid


def kernel(
    xz_h, cs_h, ssm_h, cw_h, cb_h, xp_h, gain_h, dtp_h, dtb_h, alog_h, dskip_h,
    q_h, nkv_h, pool_h, sel_h, len_h,
    mamba_h, state_h, attn_h,
    xz_v, cs_v, ssm_v, cw_v, cb_v, xp_v, gain_v, dtp_v, dtb_v, alog_v, dskip_v,
    q_v, nkv_v, pool_v, sel_s, len_s,
    mamba_v, state_v, attn_v,
    q_all, q_own, cnt_send, cnt_all, scores,
    y_send, y_recv, z_send, z_recv, g_recv, p_send, p_recv, yout,
    load_sem, out_sem,
    q_ss, q_rs, c_ss, c_rs, y_ss, y_rs, z_ss, z_rs, g_ss, g_rs, p_ss, p_rs,
):
    r = lax.axis_index("req")
    h = lax.axis_index("head")
    c = lax.axis_index("ctx")

    def zpeer(i):
        return (r, h, lax.rem(c + i, NZ))

    def ypeer(i):
        return (r, lax.rem(h + i, NY), c)

    barrier = pltpu.get_barrier_semaphore()
    for i in Z_ORDER:
        pl.semaphore_signal(barrier, inc=1, device_id=zpeer(i), device_id_type=MESH)
    for i in range(1, NY):
        pl.semaphore_signal(barrier, inc=1, device_id=ypeer(i), device_id_type=MESH)

    pairs = (
        (q_h, q_v), (sel_h, sel_s), (len_h, len_s), (xz_h, xz_v), (cs_h, cs_v), (cw_h, cw_v), (cb_h, cb_v),
        (xp_h, xp_v), (nkv_h, nkv_v), (pool_h, pool_v), (dtp_h, dtp_v), (gain_h, gain_v),
        (dtb_h, dtb_v), (alog_h, alog_v), (dskip_h, dskip_v), (ssm_h, ssm_v),
    )
    loads = [pltpu.make_async_copy(a, b, load_sem.at[k]) for k, (a, b) in enumerate(pairs)]
    for cp in loads:
        cp.start()

    loads[0].wait()
    qrow = q_v[0:1, :].astype(F32)
    for k in range(16):
        q_own[k : k + 1, :] = qrow[:, k * HEAD_DIM : (k + 1) * HEAD_DIM]
    q_all[c] = q_own[...].astype(BF16)

    loads[1].wait()
    loads[2].wait()
    shard_id = lax.broadcasted_iota(jnp.int32, (NZ, 128), 0)
    slot_id = lax.broadcasted_iota(jnp.int32, (NZ, 128), 1)
    entry = jnp.where(slot_id < POOL, shard_id * POOL + slot_id, -1)
    count = jnp.zeros((NZ, 128), jnp.int32)
    for k in range(TOPK):
        amount = len_s[0, 0] if k == 0 else PAGE
        count = jnp.where(entry == sel_s[0, k], amount, count)
    cnt_send[:, 0, :] = count.astype(F32)
    cnt_all[c] = cnt_send[c]

    for k in (3, 4, 5, 6):
        loads[k].wait()
    conv = cb_v[0:1, :] + cw_v[3:4, :] * xz_v[:, 0, :].astype(F32)
    for k in range(3):
        conv = conv + cw_v[k : k + 1, :] * cs_v[k].astype(F32)
    mixed_bf = silu(conv).astype(BF16)
    loads[7].wait()
    nt = (((1,), (1,)), ((), ()))
    for j in range(5):
        rows = 128 if j < 4 else 2 * STATE
        part = lax.dot_general(mixed_bf, xp_v[j * 128 : j * 128 + rows, :], nt, preferred_element_type=F32)
        if j == 4:
            part = jnp.concatenate([part, jnp.zeros((16, 128 - rows), F32)], axis=1)
        for k in range(NY):
            y_send[k, j] = part[4 * k : 4 * k + 4, :]

    pl.semaphore_wait(barrier, NZ - 1 + NY - 1)

    def remote(src, dst, ss, rs, k, dev):
        cp = pltpu.make_async_remote_copy(
            src_ref=src, dst_ref=dst, send_sem=ss.at[k], recv_sem=rs.at[k], device_id=dev, device_id_type=MESH
        )
        cp.start()
        return cp

    y_cp = [
        remote(y_send.at[lax.rem(h + i, NY)], y_recv.at[i - 1], y_ss, y_rs, i - 1, ypeer(i)) for i in range(1, NY)
    ]
    q_cp = [remote(q_all.at[c], q_all.at[c], q_ss, q_rs, i - 1, zpeer(i)) for i in Z_ORDER]
    c_cp = [
        remote(cnt_send.at[lax.rem(c + i, NZ)], cnt_all.at[c], c_ss, c_rs, i - 1, zpeer(i)) for i in Z_ORDER
    ]

    loads[8].wait()
    nkv = nkv_v[0:1, :].astype(F32)
    half = lax.broadcasted_iota(jnp.int32, (16, HEAD_DIM), 0) < 8
    own_key = jnp.where(half, nkv[:, 0:128], nkv[:, 256:384])
    own_value = jnp.where(half, nkv[:, 128:256], nkv[:, 384:512])
    own_score = jnp.sum(q_own[...] * own_key, axis=1, keepdims=True) * SCALE2
    tokens = POOL * PAGE
    spread = (
        lax.broadcasted_iota(jnp.int32, (128, tokens), 0)
        == lax.broadcasted_iota(jnp.int32, (128, tokens), 1) // PAGE
    ).astype(BF16)
    token_id = lax.rem(lax.broadcasted_iota(jnp.int32, (1, tokens), 1), PAGE).astype(F32)
    for k in range(9, 16):
        loads[k].wait()

    total = y_send[h]
    for i in range(NY - 1):
        y_cp[i].wait_recv()
        total = total + y_recv[i]
    z_send[...] = total
    z_cp = [remote(z_send, z_recv.at[i - 1], z_ss, z_rs, i - 1, zpeer(i)) for i in Z_ORDER]

    for cp in q_cp:
        cp.wait_recv()
    for cp in c_cp:
        cp.wait_recv()
    counts = cnt_all[:, 0, :].astype(BF16)
    limit = jnp.dot(counts, spread, preferred_element_type=F32)
    bias = jnp.where(token_id < limit, 0.0, FAR_BELOW)
    queries = q_all[...].astype(F32)
    lane = lax.broadcasted_iota(jnp.int32, (NZ, 8, HEAD_DIM), 2)
    for v in range(2):
        qv = queries[:, 8 * v : 8 * v + 8, :].reshape(NZ * 8, HEAD_DIM).astype(BF16)
        keys = pool_v[:, :, 256 * v : 256 * v + 128].reshape(tokens, HEAD_DIM)
        values = pool_v[:, :, 256 * v + 128 : 256 * v + 256].reshape(tokens, HEAD_DIM)
        s = lax.dot_general(qv, keys, nt, preferred_element_type=F32) * SCALE2
        s = s.reshape(NZ, 8, tokens) + bias[:, None, :]
        top = jnp.maximum(jnp.max(s, axis=2, keepdims=True), FLOOR)
        w = jnp.exp2(s - top).astype(BF16)
        weight_sum = jnp.sum(w.astype(F32), axis=2, keepdims=True)
        o = jnp.dot(w.reshape(NZ * 8, tokens), values, preferred_element_type=F32).reshape(NZ, 8, HEAD_DIM)
        kept = jnp.maximum(weight_sum, 1.0)
        o = o / kept
        lse = top + jnp.log2(kept)
        hi, mid, low = split3(lse)
        stat = jnp.where(lane == 0, hi, jnp.where(lane == 1, mid, jnp.where(lane == 2, low, 0.0)))
        scores[0, :, 8 * v : 8 * v + 8, :] = o
        scores[1, :, 8 * v : 8 * v + 8, :] = stat
    p_send[:, 0:16, :] = scores[0].astype(BF16)
    p_send[:, 16:32, :] = scores[1].astype(BF16)
    p_cp = [
        remote(p_send.at[lax.rem(c + i, NZ)], p_recv.at[i - 1], p_ss, p_rs, i - 1, zpeer(i)) for i in Z_ORDER
    ]

    total = z_send[...]
    for cp in z_cp:
        cp.wait_recv()
    for i in range(NZ - 1):
        total = total + z_recv[i]
    low_part = total[0:4]
    square = jnp.sum(jnp.sum(low_part * low_part, axis=0), axis=1, keepdims=True) * (1.0 / DT_RANK)
    inv = lax.rsqrt(square + EPS)
    for j in range(4):
        g_recv[h, j] = total[j] * inv * gain_v[0:1, j * 128 : (j + 1) * 128]
    g_recv[h, 4] = total[4]
    g_cp = [remote(g_recv.at[h], g_recv.at[h], g_ss, g_rs, i - 1, ypeer(i)) for i in range(1, NY)]
    rate = jnp.exp(alog_v[...])
    gate = silu(xz_v[:, 1, :].astype(F32))
    mixed = mixed_bf.astype(F32)
    for cp in g_cp:
        cp.wait_recv()

    step = dtb_v[0:1, :]
    for j in range(4):
        normed = jnp.concatenate([g_recv[k, j] for k in range(NY)], axis=0).astype(BF16)
        step = step + jnp.dot(normed, dtp_v[j * 128 : (j + 1) * 128, :], preferred_element_type=F32)
    step = jnp.maximum(step, 0.0) + jnp.log1p(jnp.exp(-jnp.abs(step)))
    terms = jnp.concatenate([g_recv[k, 4] for k in range(NY)] + [jnp.zeros((112, 128), F32)], axis=0).T
    drive = step * mixed
    for i in range(16):
        decay = jnp.exp(-(step[i : i + 1, :] * rate))
        new = decay * ssm_v[i] + drive[i : i + 1, :] * terms[0:16, i : i + 1]
        state_v[i] = new
        yout[i : i + 1, :] = jnp.sum(terms[16:32, i : i + 1] * new, axis=0, keepdims=True)
    out_state = pltpu.make_async_copy(state_v, state_h, out_sem.at[0])
    out_state.start()
    mamba_v[...] = ((yout[...] + dskip_v[0:1, :] * mixed) * gate).astype(BF16)
    out_mamba = pltpu.make_async_copy(mamba_v, mamba_h, out_sem.at[1])
    out_mamba.start()

    for cp in p_cp:
        cp.wait_recv()
    parts = [p_send[c]] + [p_recv[i] for i in range(NZ - 1)]
    levels = [jnp.sum(x[16:32, :].astype(F32), axis=1, keepdims=True) for x in parts]
    top = own_score
    for x in levels:
        top = jnp.maximum(top, x)
    weight = jnp.exp2(own_score - top)
    summed = weight * own_value
    for x, level in zip(parts, levels):
        w = jnp.exp2(level - top)
        summed = summed + w * x[0:16, :].astype(F32)
        weight = weight + w
    attn_v[...] = (summed / weight).astype(BF16)
    out_attn = pltpu.make_async_copy(attn_v, attn_h, out_sem.at[2])
    out_attn.start()

    for cp in y_cp + q_cp + c_cp + z_cp + g_cp + p_cp:
        cp.wait_send()
    out_state.wait()
    out_mamba.wait()
    out_attn.wait()


def on_device(
    xz, conv_state, ssm_state, conv_weight, conv_bias, x_proj, dt_norm_gain, dt_proj, dt_bias, a_log, d_skip,
    query, new_kv, kv_pool, page_sel, lengths,
):
    args = (
        xz, conv_state.transpose(1, 0, 2), ssm_state, conv_weight, conv_bias.reshape(1, -1), x_proj.T,
        dt_norm_gain.reshape(1, -1), dt_proj, dt_bias.reshape(1, -1), a_log, d_skip.reshape(1, -1),
        query, new_kv, kv_pool, page_sel, lengths.reshape(1, 1),
    )
    hbm = pl.BlockSpec(memory_space=pltpu.HBM)
    outs = (
        jax.ShapeDtypeStruct((16, 256), BF16),
        jax.ShapeDtypeStruct((16, STATE, 256), F32),
        jax.ShapeDtypeStruct((16, HEAD_DIM), BF16),
    )
    in_smem = {14, 15}
    scratch = [
        (pltpu.SMEM if k in in_smem else pltpu.VMEM)(a.shape, a.dtype) for k, a in enumerate(args)
    ]
    scratch += [pltpu.VMEM(o.shape, o.dtype) for o in outs]
    scratch += [
        pltpu.VMEM((NZ, 16, HEAD_DIM), BF16),
        pltpu.VMEM((16, HEAD_DIM), F32),
        pltpu.VMEM((NZ, 1, 128), F32),
        pltpu.VMEM((NZ, 1, 128), F32),
        pltpu.VMEM((2, NZ, 16, HEAD_DIM), F32),
        pltpu.VMEM((NY, 5, 4, 128), F32),
        pltpu.VMEM((NY - 1, 5, 4, 128), F32),
        pltpu.VMEM((5, 4, 128), F32),
        pltpu.VMEM((NZ - 1, 5, 4, 128), F32),
        pltpu.VMEM((NY, 5, 4, 128), F32),
        pltpu.VMEM((NZ, 32, HEAD_DIM), BF16),
        pltpu.VMEM((NZ - 1, 32, HEAD_DIM), BF16),
        pltpu.VMEM((16, 256), F32),
        pltpu.SemaphoreType.DMA((len(args),)),
        pltpu.SemaphoreType.DMA((3,)),
    ]
    for n in (NZ - 1, NZ - 1, NY - 1, NZ - 1, NY - 1, NZ - 1):
        scratch += [pltpu.SemaphoreType.DMA((n,)), pltpu.SemaphoreType.DMA((n,))]
    mamba_out, new_state, attention = pl.pallas_call(
        kernel,
        out_shape=outs,
        in_specs=[hbm] * len(args),
        out_specs=[hbm] * 3,
        scratch_shapes=scratch,
        name="decode_step",
        compiler_params=pltpu.CompilerParams(
            collective_id=0, has_side_effects=True, vmem_limit_bytes=40 * 2**20
        ),
    )(*args)
    return mamba_out, new_state, attention.reshape(1, 16 * HEAD_DIM)


def solution(mesh):
    placed = (
        P("req", None, ("head", "ctx")),
        P("req", None, ("head", "ctx")),
        P("req", None, ("head", "ctx")),
        P(None, ("head", "ctx")),
        P(("head", "ctx")),
        P(("head", "ctx"), None),
        P(),
        P(None, ("head", "ctx")),
        P(("head", "ctx")),
        P(None, ("head", "ctx")),
        P(("head", "ctx")),
        P(("req", "ctx"), "head"),
        P(("req", "ctx"), "head"),
        P(("req", "ctx"), None, "head"),
        P(("req", "ctx"), None),
        P(("req", "ctx")),
    )
    return jax.shard_map(
        on_device,
        mesh=mesh,
        in_specs=placed,
        out_specs=(
            P("req", ("head", "ctx")),
            P("req", None, ("head", "ctx")),
            P(("req", "ctx"), "head"),
        ),
        check_vma=False,
    )
```

time: 469 us -> 50.8 us (0.11)
  blocking collectives: 433 us -> 0 us
  Pallas kernels: 0 us -> 35.2 us
  starting transfers between devices: 6.91 us -> 0 us
  other arithmetic: 6.59 us -> 0 us
    psum x1 -> x0, blocking collectives: 398 us -> none  [on_device(): lax.psum(jnp.dot(mixed_bf, x_proj, preferred_element_type=jnp.float32), (...]
    all_gather x1 -> x0, blocking collectives: 35.5 us -> none  [on_device(): listed = lax.all_gather(page_sel, 'ctx', axis=0, tiled=True)]
    pallas_call x0 -> x1, Pallas kernels: none -> 35.2 us  [on_device(): pl.pallas_call(kernel, out_shape=outs, in_specs=[hbm] * len(args), out_sp...]
    unnamed x32 -> x33, local copies, waits for them, and re-layouts: 0.1 us -> 13.7 us
    slice x4 -> x0, local copies, waits for them, and re-layouts: 8.19 us -> none  [the longest x1 8.08 us: on_device(): incoming[..., 0, :]]
    all_to_all x1 -> x0, starting transfers between devices: 6.91 us -> none  [on_device(): lax.all_to_all(outgoing, 'ctx', split_axis=0, concat_axis=0, tiled=True)]
    reshape x1 -> x0, local copies, waits for them, and re-layouts: 5.5 us -> none  [on_device(): incoming.reshape(ctx_count, local_rows, MOST, PAGE, kv_local, 2, HEAD_DIM)]
  transfers between devices with their start and end apart: 1 -> 0, of which waited for: 0 -> 0; matrix products, arithmetic and copies ran while one was open for 1% -> 0% of each run, Pallas kernels for 0% -> 0%
where the time goes in v1:
time: 50.8 us; the launch traced here: 50.2 us
  Pallas kernels  35.2 us (69%)
  local copies, waits for them, and re-layouts  13.7 us (27%)
  between operations  1.32 us (3%)
    pallas_call x1, Pallas kernels, on_device(): pl.pallas_call(kernel, out_shape=outs, in_specs=[hbm] * len(args), out_sp...  35.2 us
    unnamed x33, local copies, waits for them, and re-layouts  13.7 us

profile of v1, /device:TPU:6, one launch (start us, length us, event | category | flops | bytes accessed | tf_op | source)
XLA Modules:
  0.0 50.2 jit_solution(156246665953872322)
XLA Ops:
  1.3 0.0 copy-start
  1.3 1.3 %copy-done = bf16[20,64,512]{2,1,0:T(8,128)(2,1)S(1)} copy-done((bf16[20,64,512]{2,1,0:T(8,128)(2,1)S(1)}, bf16[20,64,512]{2,1,0:T(8,128)(2,1)}, u32[]{:S(2)}) %copy-start) | copy-done | bytes 1310744
  2.6 0.0 copy-start.1
  2.6 1.0 %copy-done.1 = bf16[256,544]{0,1:T(8,128)(2,1)S(1)} copy-done((bf16[256,544]{0,1:T(8,128)(2,1)S(1)}, bf16[256,544]{0,1:T(8,128)(2,1)}, u32[]{:S(2)}) %copy-start.1) | copy-done | bytes 278552
  3.6 0.0 copy-start.2
  3.6 0.9 %copy-done.2 = f32[16,16,256]{2,1,0:T(8,128)S(1)} copy-done((f32[16,16,256]{2,1,0:T(8,128)S(1)}, f32[16,16,256]{2,1,0:T(8,128)}, u32[]{:S(2)}) %copy-start.2) | copy-done | bytes 262168
  4.5 0.0 copy-start.3
  4.5 0.9 %copy-done.3 = bf16[512,256]{1,0:T(8,128)(2,1)S(1)} copy-done((bf16[512,256]{1,0:T(8,128)(2,1)S(1)}, bf16[512,256]{1,0:T(8,128)(2,1)}, u32[]{:S(2)}) %copy-start.3) | copy-done | bytes 262168
  5.5 0.0 copy-start.4
  5.5 0.7 %copy-done.4 = bf16[16,3,256]{2,0,1:T(8,128)(2,1)S(1)} copy-done((bf16[16,3,256]{2,0,1:T(8,128)(2,1)S(1)}, bf16[16,3,256]{2,0,1:T(8,128)(2,1)}, u32[]{:S(2)}) %copy-start.4) | copy-done | bytes 24600
  6.2 0.0 copy-start.5
  6.2 0.7 %copy-done.5 = bf16[16,2,256]{2,1,0:T(2,128)(2,1)S(1)} copy-done((bf16[16,2,256]{2,1,0:T(2,128)(2,1)S(1)}, bf16[16,2,256]{2,1,0:T(2,128)(2,1)}, u32[]{:S(2)}) %copy-start.5) | copy-done | bytes 16408
  6.9 0.0 copy-start.6
  6.9 0.7 %copy-done.6 = f32[16,256]{1,0:T(8,128)S(1)} copy-done((f32[16,256]{1,0:T(8,128)S(1)}, f32[16,256]{1,0:T(8,128)}, u32[]{:S(2)}) %copy-start.6) | copy-done | bytes 16408
  7.6 0.0 copy-start.7
  7.6 0.7 %copy-done.7 = bf16[1,2048]{1,0:T(2,128)(2,1)S(1)} copy-done((bf16[1,2048]{1,0:T(2,128)(2,1)S(1)}, bf16[1,2048]{1,0:T(2,128)(2,1)}, u32[]{:S(2)}) %copy-start.7) | copy-done | bytes 4120
  8.3 0.0 copy-start.8
  8.3 0.7 %copy-done.8 = f32[4,256]{1,0:T(4,128)S(1)} copy-done((f32[4,256]{1,0:T(4,128)S(1)}, f32[4,256]{1,0:T(4,128)}, u32[]{:S(2)}) %copy-start.8) | copy-done | bytes 4120
  9.0 0.0 copy-start.9
  9.0 0.7 %copy-done.9 = f32[512]{0:T(512)S(1)} copy-done((f32[512]{0:T(512)S(1)}, f32[512]{0:T(512)}, u32[]{:S(2)}) %copy-start.9) | copy-done | bytes 2072
  9.7 0.0 copy-start.10
  9.7 0.7 %copy-done.10 = bf16[1,512]{1,0:T(2,128)(2,1)S(1)} copy-done((bf16[1,512]{1,0:T(2,128)(2,1)S(1)}, bf16[1,512]{1,0:T(2,128)(2,1)}, u32[]{:S(2)}) %copy-start.10) | copy-done | bytes 1048
  10.4 0.0 copy-start.11
  10.4 0.7 %copy-done.11 = f32[256]{0:T(256)S(1)} copy-done((f32[256]{0:T(256)S(1)}, f32[256]{0:T(256)}, u32[]{:S(2)}) %copy-start.11) | copy-done | bytes 1048
  11.1 0.0 copy-start.12
  11.1 0.7 %copy-done.12 = f32[256]{0:T(256)S(1)} copy-done((f32[256]{0:T(256)S(1)}, f32[256]{0:T(256)}, u32[]{:S(2)}) %copy-start.12) | copy-done | bytes 1048
  11.7 0.0 copy-start.13
  11.7 0.7 %copy-done.13 = f32[256]{0:T(256)S(1)} copy-done((f32[256]{0:T(256)S(1)}, f32[256]{0:T(256)}, u32[]{:S(2)}) %copy-start.13) | copy-done | bytes 1048
  12.4 0.0 copy-start.14
  12.4 0.7 %copy-done.14 = s32[1,16]{1,0:T(1,128)S(1)} copy-done((s32[1,16]{1,0:T(1,128)S(1)}, s32[1,16]{1,0:T(1,128)}, u32[]{:S(2)}) %copy-start.14) | copy-done | bytes 88
  13.1 35.2 %decode_step.1 = (bf16[16,256]{1,0:T(8,128)(2,1)S(1)}, f32[16,16,256]{2,1,0:T(8,128)S(1)}, bf16[16,128]{1,0:T(8,128)(2,1)S(1)}) custom-call(bf16[16,2,256]{2,1,0:T(2,128)(2,1)S(1)} %copy-done.5, bf16[3,16,256]{2,1,0:T(8,128)(2,1)S(1)} %bitcast.14, f32[16,16,256]{2,1,0:T(8,128)S(1)} %copy-done.2, f32[4,256]{1,0:T(4,128)S(1)} %copy-done.8, ...), custom_call_target="tpu_custom_call" | custom-call | tf_op jit(solution)/shard_map/decode_step/pallas_call | solution.py:284
  48.3 0.6 %copy.21 = bf16[1,1,16,128]{3,1,2,0:T(2,128)(2,1)} copy(bf16[1,1,16,128]{3,2,1,0:T(8,128)(2,1)S(1)} %bitcast.15) | data formatting | bytes 8192
  48.9 0.6 %copy.25 = bf16[16,256]{1,0:T(8,128)(2,1)} copy(bf16[16,256]{1,0:T(8,128)(2,1)S(1)} %get-tuple-element.12) | data formatting | bytes 16384
  49.5 0.7 %copy.26 = f32[16,16,256]{2,1,0:T(8,128)} copy(f32[16,16,256]{2,1,0:T(8,128)S(1)} %get-tuple-element.13) | data formatting | bytes 524288
Async XLA Ops:
  1.3 1.3 %copy-start = (bf16[20,64,512]{2,1,0:T(8,128)(2,1)S(1)}, bf16[20,64,512]{2,1,0:T(8,128)(2,1)}, u32[]{:S(2)}) copy-start(bf16[20,64,512]{2,1,0:T(8,128)(2,1)} %pool_h.1) | copy-start | bytes 3932164
  2.6 1.0 %copy-start.1 = (bf16[256,544]{0,1:T(8,128)(2,1)S(1)}, bf16[256,544]{0,1:T(8,128)(2,1)}, u32[]{:S(2)}) copy-start(bf16[256,544]{0,1:T(8,128)(2,1)} %param.21) | copy-start | bytes 835588
  3.6 0.9 %copy-start.2 = (f32[16,16,256]{2,1,0:T(8,128)S(1)}, f32[16,16,256]{2,1,0:T(8,128)}, u32[]{:S(2)}) copy-start(f32[16,16,256]{2,1,0:T(8,128)} %ssm_h.1) | copy-start | bytes 786436
  4.5 0.9 %copy-start.3 = (bf16[512,256]{1,0:T(8,128)(2,1)S(1)}, bf16[512,256]{1,0:T(8,128)(2,1)}, u32[]{:S(2)}) copy-start(bf16[512,256]{1,0:T(8,128)(2,1)} %dtp_h.1) | copy-start | bytes 786436
  5.5 0.7 %copy-start.4 = (bf16[16,3,256]{2,0,1:T(8,128)(2,1)S(1)}, bf16[16,3,256]{2,0,1:T(8,128)(2,1)}, u32[]{:S(2)}) copy-start(bf16[16,3,256]{2,0,1:T(8,128)(2,1)} %param.17) | copy-start | bytes 73732
  6.2 0.7 %copy-start.5 = (bf16[16,2,256]{2,1,0:T(2,128)(2,1)S(1)}, bf16[16,2,256]{2,1,0:T(2,128)(2,1)}, u32[]{:S(2)}) copy-start(bf16[16,2,256]{2,1,0:T(2,128)(2,1)} %xz_h.1) | copy-start | bytes 49156
  6.9 0.7 %copy-start.6 = (f32[16,256]{1,0:T(8,128)S(1)}, f32[16,256]{1,0:T(8,128)}, u32[]{:S(2)}) copy-start(f32[16,256]{1,0:T(8,128)} %alog_h.1) | copy-start | bytes 49156
  7.6 0.7 %copy-start.7 = (bf16[1,2048]{1,0:T(2,128)(2,1)S(1)}, bf16[1,2048]{1,0:T(2,128)(2,1)}, u32[]{:S(2)}) copy-start(bf16[1,2048]{1,0:T(2,128)(2,1)} %q_h.1) | copy-start | bytes 12292
  8.3 0.7 %copy-start.8 = (f32[4,256]{1,0:T(4,128)S(1)}, f32[4,256]{1,0:T(4,128)}, u32[]{:S(2)}) copy-start(f32[4,256]{1,0:T(4,128)} %cw_h.1) | copy-start | bytes 12292
  9.0 0.7 %copy-start.9 = (f32[512]{0:T(512)S(1)}, f32[512]{0:T(512)}, u32[]{:S(2)}) copy-start(f32[512]{0:T(512)} %param.22) | copy-start | bytes 6148
  9.7 0.7 %copy-start.10 = (bf16[1,512]{1,0:T(2,128)(2,1)S(1)}, bf16[1,512]{1,0:T(2,128)(2,1)}, u32[]{:S(2)}) copy-start(bf16[1,512]{1,0:T(2,128)(2,1)} %nkv_h.1) | copy-start | bytes 3076
  10.4 0.7 %copy-start.11 = (f32[256]{0:T(256)S(1)}, f32[256]{0:T(256)}, u32[]{:S(2)}) copy-start(f32[256]{0:T(256)} %param.20) | copy-start | bytes 3076
  11.1 0.7 %copy-start.12 = (f32[256]{0:T(256)S(1)}, f32[256]{0:T(256)}, u32[]{:S(2)}) copy-start(f32[256]{0:T(256)} %param.24) | copy-start | bytes 3076
  11.7 0.7 %copy-start.13 = (f32[256]{0:T(256)S(1)}, f32[256]{0:T(256)}, u32[]{:S(2)}) copy-start(f32[256]{0:T(256)} %param.26) | copy-start | bytes 3076
  12.4 0.7 %copy-start.14 = (s32[1,16]{1,0:T(1,128)S(1)}, s32[1,16]{1,0:T(1,128)}, u32[]{:S(2)}) copy-start(s32[1,16]{1,0:T(1,128)} %sel_h.1) | copy-start | bytes 196

commit v2 on v1

v2 whole, which is shorter than its diff:
```python
import functools
import math

import jax
import jax.numpy as jnp
from jax import lax
from jax.experimental import pallas as pl
from jax.experimental.pallas import tpu as pltpu
from jax.sharding import PartitionSpec as P

MESH = pl.DeviceIdType.MESH
STATE = 16
DT_RANK = 512
Q_HEADS = 64
KV_HEADS = 8
HEAD_DIM = 128
PAGE = 64
NZ = 16
NY = 4
POOL = 20
TOPK = 16
EPS = 1e-06
FAR_BELOW = -1e30
FLOOR = -1e29
F32 = jnp.float32
BF16 = jnp.bfloat16

SLOTS = (0, 1, 15, 2, 14, 3, 13, 4, 12, 5, 11, 6, 10, 7, 9, 8)
SLOT_OF = {i: k for k, i in enumerate(SLOTS)}
FAR_FIRST = SLOTS[:0:-1]
GROUPS = ((0, 8), (8, 16))
SCALE2 = math.log2(math.e) / math.sqrt(HEAD_DIM)
NT = (((1,), (1,)), ((), ()))


def silu(v):
    return v / (1.0 + jnp.exp(-v))


def kernel(
    xz_h, cs_h, ssm_h, cw_h, cb_h, xp_h, gain_h, dtp_h, dtb_h, alog_h, dskip_h,
    q_h, nkv_h, pool_h, sel_h, len_h,
    mamba_v, state_v, attn_v,
    xz_v, cs_v, ssm_v, cw_v, cb_v, xp_v, gain_v, dtp_v, dtb_v, alog_v, dskip_v,
    q_v, nkv_v, pool_v, sel_s, len_s,
    q_own, q_all, cnt_send, cnt_all, y_send, y_recv, z_send, zb_send, z_recv, zb_recv, g_recv,
    p_send, pl_send, p_recv, pl_recv, yout,
    load_sem, q_ss, q_rs, c_ss, c_rs, y_ss, y_rs, z_ss, z_rs, zb_ss, zb_rs, g_ss, g_rs, p_ss, p_rs, pl_ss, pl_rs,
):
    r = lax.axis_index("req")
    h = lax.axis_index("head")
    c = lax.axis_index("ctx")

    def zpeer(i):
        return (r, h, lax.rem(c + i, NZ))

    def ypeer(i):
        return (r, lax.rem(h + i, NY), c)

    started = []

    def remote(src, dst, ss, rs, k, dev):
        cp = pltpu.make_async_remote_copy(
            src_ref=src, dst_ref=dst, send_sem=ss.at[k], recv_sem=rs.at[k], device_id=dev, device_id_type=MESH
        )
        cp.start()
        started.append(cp)
        return cp

    barrier = pltpu.get_barrier_semaphore()
    for i in FAR_FIRST:
        pl.semaphore_signal(barrier, inc=1, device_id=zpeer(i), device_id_type=MESH)
    for i in range(1, NY):
        pl.semaphore_signal(barrier, inc=1, device_id=ypeer(i), device_id_type=MESH)

    pairs = (
        (q_h, q_v), (sel_h, sel_s), (len_h, len_s), (xz_h, xz_v), (cs_h, cs_v), (cw_h, cw_v), (cb_h, cb_v),
        (xp_h, xp_v), (nkv_h, nkv_v), (pool_h, pool_v), (dtp_h, dtp_v), (gain_h, gain_v),
        (dtb_h, dtb_v), (alog_h, alog_v), (dskip_h, dskip_v), (ssm_h, ssm_v),
    )
    loads = [pltpu.make_async_copy(a, b, load_sem.at[k]) for k, (a, b) in enumerate(pairs)]
    for cp in loads:
        cp.start()

    loads[0].wait()
    qrow = q_v[0:1, :].astype(F32)
    for k in range(16):
        q_own[k : k + 1, :] = qrow[:, k * HEAD_DIM : (k + 1) * HEAD_DIM]
    q_all[0] = q_own[...].astype(BF16)

    loads[1].wait()
    loads[2].wait()
    shard_id = lax.broadcasted_iota(jnp.int32, (NZ, 128), 0)
    slot_id = lax.broadcasted_iota(jnp.int32, (NZ, 128), 1)
    entry = jnp.where(slot_id < POOL, shard_id * POOL + slot_id, -1)
    count = jnp.zeros((NZ, 128), jnp.int32)
    for k in range(TOPK):
        amount = len_s[0, 0] if k == 0 else PAGE
        count = jnp.where(entry == sel_s[0, k], amount, count)
    cnt_send[:, 0, :] = count.astype(F32)
    cnt_all[0] = cnt_send[c]

    for k in (3, 4, 5, 6):
        loads[k].wait()
    conv = cb_v[0:1, :] + cw_v[3:4, :] * xz_v[:, 0, :].astype(F32)
    for k in range(3):
        conv = conv + cw_v[k : k + 1, :] * cs_v[k].astype(F32)
    mixed_bf = silu(conv).astype(BF16)
    loads[7].wait()
    for j in range(4):
        part = lax.dot_general(mixed_bf, xp_v[j * 128 : (j + 1) * 128, :], NT, preferred_element_type=F32)
        for k in range(NY):
            y_send[k, 4 * j : 4 * j + 4, :] = part[4 * k : 4 * k + 4, :]
    part = lax.dot_general(mixed_bf, xp_v[DT_RANK : DT_RANK + 32, :], NT, preferred_element_type=F32)
    for k in range(NY):
        y_send[k, 16:17, :] = jnp.concatenate([part[4 * k + i : 4 * k + i + 1, :] for i in range(4)], axis=1)

    pl.semaphore_wait(barrier, NZ - 1 + NY - 1)

    y_cp = [
        remote(y_send.at[lax.rem(h + i, NY)], y_recv.at[i - 1], y_ss, y_rs, i - 1, ypeer(i)) for i in range(1, NY)
    ]
    q_cp, c_cp = {}, {}
    for i in FAR_FIRST:
        q_cp[i] = remote(q_all.at[0], q_all.at[SLOT_OF[i]], q_ss, q_rs, i - 1, zpeer(i))
        c_cp[i] = remote(
            cnt_send.at[lax.rem(c + i, NZ)], cnt_all.at[SLOT_OF[i]], c_ss, c_rs, i - 1, zpeer(i)
        )

    loads[8].wait()
    nkv = nkv_v[0:1, :].astype(F32)
    half = lax.broadcasted_iota(jnp.int32, (16, HEAD_DIM), 0) < 8
    own_key = jnp.where(half, nkv[:, 0:128], nkv[:, 256:384])
    own_value = jnp.where(half, nkv[:, 128:256], nkv[:, 384:512])
    own_score = jnp.sum(q_own[...] * own_key, axis=1, keepdims=True) * SCALE2
    tokens = POOL * PAGE
    spread = (
        lax.broadcasted_iota(jnp.int32, (128, tokens), 0)
        == lax.broadcasted_iota(jnp.int32, (128, tokens), 1) // PAGE
    ).astype(BF16)
    token_id = lax.rem(lax.broadcasted_iota(jnp.int32, (1, tokens), 1), PAGE).astype(F32)
    for k in range(9, 16):
        loads[k].wait()
    gain = jnp.concatenate(
        [jnp.broadcast_to(gain_v[0:1, j * 128 : (j + 1) * 128], (4, 128)) for j in range(4)], axis=0
    )

    total = y_send[h]
    for i in range(NY - 1):
        y_cp[i].wait_recv()
        total = total + y_recv[i]
    z_send[...] = total[0:16].astype(BF16)
    zb_send[...] = total[16:17]
    z_cp, zb_cp = {}, {}
    for i in FAR_FIRST:
        z_cp[i] = remote(z_send, z_recv.at[i - 1], z_ss, z_rs, i - 1, zpeer(i))
        zb_cp[i] = remote(zb_send, zb_recv.at[i - 1], zb_ss, zb_rs, i - 1, zpeer(i))

    diagonal = (
        lax.broadcasted_iota(jnp.int32, (1, 16, HEAD_DIM), 1)
        == lax.broadcasted_iota(jnp.int32, (1, 16, HEAD_DIM), 2)
    )
    p_cp, pl_cp = {}, {}
    for first, last in GROUPS:
        n = last - first
        for i in SLOTS[first:last]:
            if i:
                c_cp[i].wait_recv()
                q_cp[i].wait_recv()
        counts = cnt_all[first:last, 0, :].astype(BF16)
        limit = jnp.dot(counts, spread, preferred_element_type=F32)
        bias = jnp.where(token_id < limit, 0.0, FAR_BELOW)
        queries = q_all[first:last].astype(F32)
        outs, levels = [], []
        for v in range(2):
            qv = queries[:, 8 * v : 8 * v + 8, :].reshape(n * 8, HEAD_DIM).astype(BF16)
            keys = pool_v[:, :, 256 * v : 256 * v + 128].reshape(tokens, HEAD_DIM)
            values = pool_v[:, :, 256 * v + 128 : 256 * v + 256].reshape(tokens, HEAD_DIM)
            s = lax.dot_general(qv, keys, NT, preferred_element_type=F32) * SCALE2
            s = s.reshape(n, 8, tokens) + bias[:, None, :]
            top = jnp.maximum(jnp.max(s, axis=2, keepdims=True), FLOOR)
            w = jnp.exp2(s - top).astype(BF16)
            weight_sum = jnp.sum(w.astype(F32), axis=2, keepdims=True)
            o = jnp.dot(w.reshape(n * 8, tokens), values, preferred_element_type=F32).reshape(n, 8, HEAD_DIM)
            kept = jnp.maximum(weight_sum, 1.0)
            outs.append(o / kept)
            levels.append(top + jnp.log2(kept))
        level = jnp.concatenate(levels, axis=1)
        p_send[first:last] = jnp.concatenate(outs, axis=1).astype(BF16)
        pl_send[first:last] = jnp.sum(jnp.where(diagonal, level, 0.0), axis=1, keepdims=True)
        for i in SLOTS[first:last][::-1]:
            if i:
                k = SLOT_OF[i]
                back = NZ - i
                p_cp[back] = remote(p_send.at[k], p_recv.at[SLOT_OF[back]], p_ss, p_rs, back - 1, zpeer(back))
                pl_cp[back] = remote(pl_send.at[k], pl_recv.at[SLOT_OF[back]], pl_ss, pl_rs, back - 1, zpeer(back))

    total = total[0:16]
    terms = zb_send[...]
    for i in SLOTS[1:]:
        z_cp[i].wait_recv()
        zb_cp[i].wait_recv()
        total = total + z_recv[i - 1].astype(F32)
        terms = terms + zb_recv[i - 1]
    square = total * total
    square = square[0:8] + square[8:16]
    square = square + jnp.concatenate([square[4:8], square[0:4]], axis=0)
    square = jnp.sum(square, axis=1, keepdims=True) * (1.0 / DT_RANK)
    inv = lax.rsqrt(square + EPS)
    g_recv[h, 0:16, :] = total * jnp.concatenate([inv, inv], axis=0) * gain
    g_recv[h, 16:17, :] = terms
    g_cp = [remote(g_recv.at[h], g_recv.at[h], g_ss, g_rs, i - 1, ypeer(i)) for i in range(1, NY)]
    rate = jnp.exp(alog_v[...])
    gate = silu(xz_v[:, 1, :].astype(F32))
    mixed = mixed_bf.astype(F32)
    for cp in g_cp:
        cp.wait_recv()

    step = dtb_v[0:1, :]
    for j in range(4):
        normed = jnp.concatenate([g_recv[k, 4 * j : 4 * j + 4, :] for k in range(NY)], axis=0).astype(BF16)
        step = step + jnp.dot(normed, dtp_v[j * 128 : (j + 1) * 128, :], preferred_element_type=F32)
    step = jnp.maximum(step, 0.0) + jnp.log1p(jnp.exp(-jnp.abs(step)))
    terms = jnp.concatenate([g_recv[k, 16:17, :] for k in range(NY)] + [jnp.zeros((124, 128), F32)], axis=0).T
    drive = step * mixed
    for i in range(16):
        k, low = i // 4, 32 * (i % 4)
        decay = jnp.exp(-(step[i : i + 1, :] * rate))
        new = decay * ssm_v[i] + drive[i : i + 1, :] * terms[low : low + 16, k : k + 1]
        state_v[i] = new
        yout[i : i + 1, :] = jnp.sum(terms[low + 16 : low + 32, k : k + 1] * new, axis=0, keepdims=True)
    mamba_v[...] = ((yout[...] + dskip_v[0:1, :] * mixed) * gate).astype(BF16)

    p_recv[0] = p_send[0]
    pl_recv[0] = pl_send[0]
    top, weight, summed = own_score, jnp.ones_like(own_score), own_value
    for first, last in GROUPS:
        for i in SLOTS[first:last]:
            if i:
                pl_cp[i].wait_recv()
                p_cp[i].wait_recv()
        level = jnp.sum(jnp.where(diagonal, pl_recv[first:last], 0.0), axis=2, keepdims=True)
        new_top = jnp.maximum(top, jnp.max(level, axis=0))
        old = jnp.exp2(top - new_top)
        w = jnp.exp2(level - new_top[None])
        weight = weight * old + jnp.sum(w, axis=0)
        summed = summed * old + jnp.sum(w * p_recv[first:last].astype(F32), axis=0)
        top = new_top
    joined = (summed / weight).astype(BF16)
    for k in range(16):
        attn_v[0:1, k * HEAD_DIM : (k + 1) * HEAD_DIM] = joined[k : k + 1, :]

    for cp in started:
        cp.wait_send()


def hand_over(a_in, b_in, c_in, a_out, b_out, c_out, sem):
    copies = [
        pltpu.make_async_copy(x, y, sem.at[k])
        for k, (x, y) in enumerate(((a_in, a_out), (b_in, b_out), (c_in, c_out)))
    ]
    for cp in copies:
        cp.start()
    for cp in copies:
        cp.wait()


def on_device(
    xz, conv_state, ssm_state, conv_weight, conv_bias, x_proj, dt_norm_gain, dt_proj, dt_bias, a_log, d_skip,
    query, new_kv, kv_pool, page_sel, lengths,
):
    args = (
        xz, conv_state.transpose(1, 0, 2), ssm_state, conv_weight, conv_bias.reshape(1, -1), x_proj.T,
        dt_norm_gain.reshape(1, -1), dt_proj, dt_bias.reshape(1, -1), a_log, d_skip.reshape(1, -1),
        query, new_kv, kv_pool, page_sel, lengths.reshape(1, 1),
    )
    hbm = pl.BlockSpec(memory_space=pltpu.HBM)
    vmem = pl.BlockSpec(memory_space=pltpu.VMEM)
    outs = (((16, 256), BF16), ((16, STATE, 256), F32), ((1, 16 * HEAD_DIM), BF16))
    in_smem = {14, 15}
    scratch = [
        (pltpu.SMEM if k in in_smem else pltpu.VMEM)(a.shape, a.dtype) for k, a in enumerate(args)
    ]
    scratch += [
        pltpu.VMEM((16, HEAD_DIM), F32),
        pltpu.VMEM((NZ, 16, HEAD_DIM), BF16),
        pltpu.VMEM((NZ, 1, 128), F32),
        pltpu.VMEM((NZ, 1, 128), F32),
        pltpu.VMEM((NY, 17, 128), F32),
        pltpu.VMEM((NY - 1, 17, 128), F32),
        pltpu.VMEM((16, 128), BF16),
        pltpu.VMEM((1, 128), F32),
        pltpu.VMEM((NZ - 1, 16, 128), BF16),
        pltpu.VMEM((NZ - 1, 1, 128), F32),
        pltpu.VMEM((NY, 17, 128), F32),
        pltpu.VMEM((NZ, 16, HEAD_DIM), BF16),
        pltpu.VMEM((NZ, 1, 128), F32),
        pltpu.VMEM((NZ, 16, HEAD_DIM), BF16),
        pltpu.VMEM((NZ, 1, 128), F32),
        pltpu.VMEM((16, 256), F32),
        pltpu.SemaphoreType.DMA((len(args),)),
    ]
    for n in (NZ - 1, NZ - 1, NY - 1, NZ - 1, NZ - 1, NY - 1, NZ - 1, NZ - 1):
        scratch += [pltpu.SemaphoreType.DMA((n,)), pltpu.SemaphoreType.DMA((n,))]
    made = pl.pallas_call(
        kernel,
        out_shape=[pltpu.VMEM(*o) for o in outs],
        in_specs=[hbm] * len(args),
        out_specs=[vmem] * 3,
        scratch_shapes=scratch,
        name="decode_step",
        compiler_params=pltpu.CompilerParams(
            collective_id=0, has_side_effects=True, vmem_limit_bytes=60 * 2**20
        ),
    )(*args)
    return pl.pallas_call(
        hand_over,
        out_shape=[jax.ShapeDtypeStruct(*o) for o in outs],
        in_specs=[vmem] * 3,
        out_specs=[hbm] * 3,
        scratch_shapes=[pltpu.SemaphoreType.DMA((3,))],
        name="hand_over",
        compiler_params=pltpu.CompilerParams(vmem_limit_bytes=4 * 2**20),
    )(*made)


def solution(mesh):
    placed = (
        P("req", None, ("head", "ctx")),
        P("req", None, ("head", "ctx")),
        P("req", None, ("head", "ctx")),
        P(None, ("head", "ctx")),
        P(("head", "ctx")),
        P(("head", "ctx"), None),
        P(),
        P(None, ("head", "ctx")),
        P(("head", "ctx")),
        P(None, ("head", "ctx")),
        P(("head", "ctx")),
        P(("req", "ctx"), "head"),
        P(("req", "ctx"), "head"),
        P(("req", "ctx"), None, "head"),
        P(("req", "ctx"), None),
        P(("req", "ctx")),
    )
    return jax.shard_map(
        on_device,
        mesh=mesh,
        in_specs=placed,
        out_specs=(
            P("req", ("head", "ctx")),
            P("req", None, ("head", "ctx")),
            P(("req", "ctx"), "head"),
        ),
        check_vma=False,
    )
```

time: 50.8 us -> 34.5 us (0.68)
  local copies, waits for them, and re-layouts: 13.7 us -> 0 us
  Pallas kernels: 35.2 us -> 33 us
    unnamed x33 -> x0, local copies, waits for them, and re-layouts: 13.7 us -> none
    pallas_call x1 -> x2, Pallas kernels: 35.2 us -> 33 us  [the longest x1 32.3 us: on_device(): pl.pallas_call(kernel, out_shape=[pltpu.VMEM(*o) for o in outs], in_specs...]
where the time goes in v2:
time: 34.5 us; the launch traced here: 34.3 us
  Pallas kernels  33 us (96%)
  between operations  1.29 us (4%)
    pallas_call x1, Pallas kernels, on_device(): pl.pallas_call(kernel, out_shape=[pltpu.VMEM(*o) for o in outs], in_specs...  32.3 us
    pallas_call x1, Pallas kernels, on_device(): pl.pallas_call(hand_over, out_shape=[jax.ShapeDtypeStruct(*o) for o in ou...  0.74 us

profile of v2, /device:TPU:6, one launch (start us, length us, event | category | flops | bytes accessed | tf_op | source)
XLA Modules:
  0.0 34.3 jit_solution(562095222333981836)
XLA Ops:
  1.3 32.3 %decode_step.1 = (bf16[16,256]{1,0:T(8,128)(2,1)S(1)}, f32[16,16,256]{2,1,0:T(8,128)S(1)}, bf16[1,2048]{1,0:T(2,128)(2,1)S(1)}) custom-call(bf16[16,2,256]{2,1,0:T(2,128)(2,1)} %xz_h.1, bf16[3,16,256]{2,1,0:T(8,128)(2,1)} %bitcast.9, f32[16,16,256]{2,1,0:T(8,128)} %ssm_h.1, f32[4,256]{1,0:T(4,128)} %cw_h.1, f32[1,256]{1,0:T(1,128)} %bitcast.11, ...), custom_call_target="tpu_custom_call" | custom-call | tf_op jit(solution)/shard_map/decode_step/pallas_call | solution.py:305
  33.6 0.7 %hand_over.1 = (bf16[16,256]{1,0:T(8,128)(2,1)}, f32[16,16,256]{2,1,0:T(8,128)}, bf16[1,2048]{1,0:T(2,128)(2,1)}) custom-call(bf16[16,256]{1,0:T(8,128)(2,1)S(1)} %get-tuple-element.6.a_in, f32[16,16,256]{2,1,0:T(8,128)S(1)} %get-tuple-element.7.b_in, bf16[1,2048]{1,0:T(2,128)(2,1)S(1)} %get-tuple-element.8.c_in), custom_call_target="tpu_custom_call" | custom-call | tf_op jit(solution)/shard_map/hand_over/pallas_call | solution.py:316

commit v3 on v2

--- a/solution.py
+++ b/solution.py
@@ -57,15 +57,19 @@
     def ypeer(i):
         return (r, lax.rem(h + i, NY), c)
 
-    started = []
-
-    def remote(src, dst, ss, rs, k, dev):
-        cp = pltpu.make_async_remote_copy(
-            src_ref=src, dst_ref=dst, send_sem=ss.at[k], recv_sem=rs.at[k], device_id=dev, device_id_type=MESH
-        )
-        cp.start()
-        started.append(cp)
-        return cp
+    def send(src, dst, ss, rs, dev):
+        pltpu.make_async_remote_copy(
+            src_ref=src, dst_ref=dst, send_sem=ss, recv_sem=rs, device_id=dev, device_id_type=MESH
+        ).start()
+
+    def drain(ref, sem):
+        pltpu.make_async_copy(ref, ref, sem).wait()
+
+    def part_of(first, last):
+        return pl.ds(max(first, 1), last - max(first, 1))
+
+    def group_of(i):
+        return next(g for g, (first, last) in enumerate(GROUPS) if first <= SLOT_OF[i] < last)
 
     barrier = pltpu.get_barrier_semaphore()
     for i in FAR_FIRST:
@@ -115,18 +119,6 @@
     for k in range(NY):
         y_send[k, 16:17, :] = jnp.concatenate([part[4 * k + i : 4 * k + i + 1, :] for i in range(4)], axis=1)
 
-    pl.semaphore_wait(barrier, NZ - 1 + NY - 1)
-
-    y_cp = [
-        remote(y_send.at[lax.rem(h + i, NY)], y_recv.at[i - 1], y_ss, y_rs, i - 1, ypeer(i)) for i in range(1, NY)
-    ]
-    q_cp, c_cp = {}, {}
-    for i in FAR_FIRST:
-        q_cp[i] = remote(q_all.at[0], q_all.at[SLOT_OF[i]], q_ss, q_rs, i - 1, zpeer(i))
-        c_cp[i] = remote(
-            cnt_send.at[lax.rem(c + i, NZ)], cnt_all.at[SLOT_OF[i]], c_ss, c_rs, i - 1, zpeer(i)
-        )
-
     loads[8].wait()
     nkv = nkv_v[0:1, :].astype(F32)
     half = lax.broadcasted_iota(jnp.int32, (16, HEAD_DIM), 0) < 8
@@ -134,42 +126,54 @@
     own_value = jnp.where(half, nkv[:, 128:256], nkv[:, 384:512])
     own_score = jnp.sum(q_own[...] * own_key, axis=1, keepdims=True) * SCALE2
     tokens = POOL * PAGE
-    spread = (
-        lax.broadcasted_iota(jnp.int32, (128, tokens), 0)
-        == lax.broadcasted_iota(jnp.int32, (128, tokens), 1) // PAGE
-    ).astype(BF16)
-    token_id = lax.rem(lax.broadcasted_iota(jnp.int32, (1, tokens), 1), PAGE).astype(F32)
+    lane = lax.broadcasted_iota(jnp.int32, (1, 128), 1)
+    low_half = lane < PAGE
+    token = jnp.where(low_half, lane, lane - PAGE).astype(F32)
     for k in range(9, 16):
         loads[k].wait()
     gain = jnp.concatenate(
         [jnp.broadcast_to(gain_v[0:1, j * 128 : (j + 1) * 128], (4, 128)) for j in range(4)], axis=0
     )
 
+    pl.semaphore_wait(barrier, NZ - 1 + NY - 1)
+
+    for i in range(1, NY):
+        send(y_send.at[lax.rem(h + i, NY)], y_recv.at[i - 1], y_ss, y_rs, ypeer(i))
+    for i in FAR_FIRST:
+        g = group_of(i)
+        send(q_all.at[0], q_all.at[SLOT_OF[i]], q_ss, q_rs.at[g], zpeer(i))
+        send(cnt_send.at[lax.rem(c + i, NZ)], cnt_all.at[SLOT_OF[i]], c_ss, c_rs.at[g], zpeer(i))
+
     total = y_send[h]
+    drain(y_recv, y_rs)
     for i in range(NY - 1):
-        y_cp[i].wait_recv()
         total = total + y_recv[i]
     z_send[...] = total[0:16].astype(BF16)
     zb_send[...] = total[16:17]
-    z_cp, zb_cp = {}, {}
     for i in FAR_FIRST:
-        z_cp[i] = remote(z_send, z_recv.at[i - 1], z_ss, z_rs, i - 1, zpeer(i))
-        zb_cp[i] = remote(zb_send, zb_recv.at[i - 1], zb_ss, zb_rs, i - 1, zpeer(i))
+        send(z_send, z_recv.at[i - 1], z_ss, z_rs, zpeer(i))
+        send(zb_send, zb_recv.at[i - 1], zb_ss, zb_rs, zpeer(i))
 
     diagonal = (
         lax.broadcasted_iota(jnp.int32, (1, 16, HEAD_DIM), 1)
         == lax.broadcasted_iota(jnp.int32, (1, 16, HEAD_DIM), 2)
     )
-    p_cp, pl_cp = {}, {}
-    for first, last in GROUPS:
+    for g, (first, last) in enumerate(GROUPS):
         n = last - first
-        for i in SLOTS[first:last]:
-            if i:
-                c_cp[i].wait_recv()
-                q_cp[i].wait_recv()
-        counts = cnt_all[first:last, 0, :].astype(BF16)
-        limit = jnp.dot(counts, spread, preferred_element_type=F32)
-        bias = jnp.where(token_id < limit, 0.0, FAR_BELOW)
+        drain(cnt_all.at[part_of(first, last)], c_rs.at[g])
+        drain(q_all.at[part_of(first, last)], q_rs.at[g])
+        counts = cnt_all[first:last, 0, :]
+        bias = jnp.concatenate(
+            [
+                jnp.where(
+                    token < jnp.where(low_half, counts[:, 2 * j : 2 * j + 1], counts[:, 2 * j + 1 : 2 * j + 2]),
+                    0.0,
+                    FAR_BELOW,
+                )
+                for j in range(POOL // 2)
+            ],
+            axis=1,
+        )
         queries = q_all[first:last].astype(F32)
         outs, levels = [], []
         for v in range(2):
@@ -190,16 +194,16 @@
         pl_send[first:last] = jnp.sum(jnp.where(diagonal, level, 0.0), axis=1, keepdims=True)
         for i in SLOTS[first:last][::-1]:
             if i:
-                k = SLOT_OF[i]
-                back = NZ - i
-                p_cp[back] = remote(p_send.at[k], p_recv.at[SLOT_OF[back]], p_ss, p_rs, back - 1, zpeer(back))
-                pl_cp[back] = remote(pl_send.at[k], pl_recv.at[SLOT_OF[back]], pl_ss, pl_rs, back - 1, zpeer(back))
+                k, back = SLOT_OF[i], NZ - i
+                slot, to = SLOT_OF[back], group_of(back)
+                send(p_send.at[k], p_recv.at[slot], p_ss, p_rs.at[to], zpeer(back))
+                send(pl_send.at[k], pl_recv.at[slot], pl_ss, pl_rs.at[to], zpeer(back))
 
     total = total[0:16]
     terms = zb_send[...]
+    drain(z_recv, z_rs)
+    drain(zb_recv, zb_rs)
     for i in SLOTS[1:]:
-        z_cp[i].wait_recv()
-        zb_cp[i].wait_recv()
         total = total + z_recv[i - 1].astype(F32)
         terms = terms + zb_recv[i - 1]
     square = total * total
@@ -209,12 +213,12 @@
     inv = lax.rsqrt(square + EPS)
     g_recv[h, 0:16, :] = total * jnp.concatenate([inv, inv], axis=0) * gain
     g_recv[h, 16:17, :] = terms
-    g_cp = [remote(g_recv.at[h], g_recv.at[h], g_ss, g_rs, i - 1, ypeer(i)) for i in range(1, NY)]
+    for i in range(1, NY):
+        send(g_recv.at[h], g_recv.at[h], g_ss, g_rs, ypeer(i))
     rate = jnp.exp(alog_v[...])
     gate = silu(xz_v[:, 1, :].astype(F32))
     mixed = mixed_bf.astype(F32)
-    for cp in g_cp:
-        cp.wait_recv()
+    drain(y_recv, g_rs)
 
     step = dtb_v[0:1, :]
     for j in range(4):
@@ -234,11 +238,9 @@
     p_recv[0] = p_send[0]
     pl_recv[0] = pl_send[0]
     top, weight, summed = own_score, jnp.ones_like(own_score), own_value
-    for first, last in GROUPS:
-        for i in SLOTS[first:last]:
-            if i:
-                pl_cp[i].wait_recv()
-                p_cp[i].wait_recv()
+    for g, (first, last) in enumerate(GROUPS):
+        drain(pl_recv.at[part_of(first, last)], pl_rs.at[g])
+        drain(p_recv.at[part_of(first, last)], p_rs.at[g])
         level = jnp.sum(jnp.where(diagonal, pl_recv[first:last], 0.0), axis=2, keepdims=True)
         new_top = jnp.maximum(top, jnp.max(level, axis=0))
         old = jnp.exp2(top - new_top)
@@ -250,8 +252,12 @@
     for k in range(16):
         attn_v[0:1, k * HEAD_DIM : (k + 1) * HEAD_DIM] = joined[k : k + 1, :]
 
-    for cp in started:
-        cp.wait_send()
+    peers = pl.ds(1, NZ - 1)
+    for ref, sem in (
+        (y_recv, y_ss), (q_all.at[peers], q_ss), (cnt_all.at[peers], c_ss), (z_recv, z_ss), (zb_recv, zb_ss),
+        (y_recv, g_ss), (p_recv.at[peers], p_ss), (pl_recv.at[peers], pl_ss),
+    ):
+        drain(ref, sem)
 
 
 def hand_over(a_in, b_in, c_in, a_out, b_out, c_out, sem):
@@ -300,8 +306,8 @@
         pltpu.VMEM((16, 256), F32),
         pltpu.SemaphoreType.DMA((len(args),)),
     ]
-    for n in (NZ - 1, NZ - 1, NY - 1, NZ - 1, NZ - 1, NY - 1, NZ - 1, NZ - 1):
-        scratch += [pltpu.SemaphoreType.DMA((n,)), pltpu.SemaphoreType.DMA((n,))]
+    one, grouped = pltpu.SemaphoreType.DMA, pltpu.SemaphoreType.DMA((len(GROUPS),))
+    scratch += [one, grouped, one, grouped, one, one, one, one, one, one, one, one, one, grouped, one, grouped]
     made = pl.pallas_call(
         kernel,
         out_shape=[pltpu.VMEM(*o) for o in outs],

time: 34.5 us -> 32.9 us (0.954)
  Pallas kernels: 33 us -> 31.4 us
    pallas_call x1, Pallas kernels: 32.3 us -> 30.7 us  [on_device(): pl.pallas_call(kernel, out_shape=[pltpu.VMEM(*o) for o in outs], in_specs...]
where the time goes in v3:
time: 32.9 us; the launch traced here: 32.7 us
  Pallas kernels  31.4 us (95%)
  between operations  1.29 us (4%)
    pallas_call x1, Pallas kernels, on_device(): pl.pallas_call(kernel, out_shape=[pltpu.VMEM(*o) for o in outs], in_specs...  30.7 us
    pallas_call x1, Pallas kernels, on_device(): pl.pallas_call(hand_over, out_shape=[jax.ShapeDtypeStruct(*o) for o in ou...  0.74 us

profile of v3, /device:TPU:6, one launch (start us, length us, event | category | flops | bytes accessed | tf_op | source)
XLA Modules:
  0.0 32.7 jit_solution(11619092474437541065)
XLA Ops:
  1.3 30.7 %decode_step.1 = (bf16[16,256]{1,0:T(8,128)(2,1)S(1)}, f32[16,16,256]{2,1,0:T(8,128)S(1)}, bf16[1,2048]{1,0:T(2,128)(2,1)S(1)}) custom-call(bf16[16,2,256]{2,1,0:T(2,128)(2,1)} %xz_h.1, bf16[3,16,256]{2,1,0:T(8,128)(2,1)} %bitcast.9, f32[16,16,256]{2,1,0:T(8,128)} %ssm_h.1, f32[4,256]{1,0:T(4,128)} %cw_h.1, f32[1,256]{1,0:T(1,128)} %bitcast.11, ...), custom_call_target="tpu_custom_call" | custom-call | tf_op jit(solution)/shard_map/decode_step/pallas_call | solution.py:311
  32.0 0.7 %hand_over.1 = (bf16[16,256]{1,0:T(8,128)(2,1)}, f32[16,16,256]{2,1,0:T(8,128)}, bf16[1,2048]{1,0:T(2,128)(2,1)}) custom-call(bf16[16,256]{1,0:T(8,128)(2,1)S(1)} %get-tuple-element.6.a_in, f32[16,16,256]{2,1,0:T(8,128)S(1)} %get-tuple-element.7.b_in, bf16[1,2048]{1,0:T(2,128)(2,1)S(1)} %get-tuple-element.8.c_in), custom_call_target="tpu_custom_call" | custom-call | tf_op jit(solution)/shard_map/hand_over/pallas_call | solution.py:322

commit v4 on v3

--- a/solution.py
+++ b/solution.py
@@ -25,10 +25,12 @@
 F32 = jnp.float32
 BF16 = jnp.bfloat16
 
-SLOTS = (0, 1, 15, 2, 14, 3, 13, 4, 12, 5, 11, 6, 10, 7, 9, 8)
-SLOT_OF = {i: k for k, i in enumerate(SLOTS)}
-FAR_FIRST = SLOTS[:0:-1]
-GROUPS = ((0, 8), (8, 16))
+FAR_FIRST = (8, 9, 7, 10, 6, 11, 5, 12, 4, 13, 3, 14, 2, 15, 1)
+EARLY = 1
+HUB = 4
+HUB_ORDER = tuple(t for t in (8, 9, 10, 12, 11, 13, 14, 7, 6, 15, 5, 4, 3, 2, 1) if t >= EARLY and t != HUB)
+GROUPS = ((0, EARLY), (EARLY, NZ))
+HALF = NZ // 2
 SCALE2 = math.log2(math.e) / math.sqrt(HEAD_DIM)
 NT = (((1,), (1,)), ((), ()))
 
@@ -43,9 +45,9 @@
     mamba_v, state_v, attn_v,
     xz_v, cs_v, ssm_v, cw_v, cb_v, xp_v, gain_v, dtp_v, dtb_v, alog_v, dskip_v,
     q_v, nkv_v, pool_v, sel_s, len_s,
-    q_own, q_all, cnt_send, cnt_all, y_send, y_recv, z_send, zb_send, z_recv, zb_recv, g_recv,
+    q_own, q_all, sel_all, y_send, y_recv, z_send, zb_send, z_recv, zb_recv, g_recv,
     p_send, pl_send, p_recv, pl_recv, yout,
-    load_sem, q_ss, q_rs, c_ss, c_rs, y_ss, y_rs, z_ss, z_rs, zb_ss, zb_rs, g_ss, g_rs, p_ss, p_rs, pl_ss, pl_rs,
+    load_sem, q_ss, q_rs, c_ss, c_rs, f_ss, fc_ss, y_ss, y_rs, z_ss, z_rs, zb_ss, zb_rs, g_ss, g_rs, p_ss, p_rs, pl_ss, pl_rs,
 ):
     r = lax.axis_index("req")
     h = lax.axis_index("head")
@@ -65,17 +67,23 @@
     def drain(ref, sem):
         pltpu.make_async_copy(ref, ref, sem).wait()
 
-    def part_of(first, last):
-        return pl.ds(max(first, 1), last - max(first, 1))
-
-    def group_of(i):
-        return next(g for g, (first, last) in enumerate(GROUPS) if first <= SLOT_OF[i] < last)
+    is_early = c < EARLY
+    is_late = c >= EARLY
+    is_hub = c == HUB
+    is_rest = is_late & (c != HUB)
+
+    def target_of(i):
+        return lax.rem(c + i, NZ)
 
     barrier = pltpu.get_barrier_semaphore()
+
+    def greet(dev):
+        pl.semaphore_signal(barrier, inc=1, device_id=dev, device_id_type=MESH)
+
     for i in FAR_FIRST:
-        pl.semaphore_signal(barrier, inc=1, device_id=zpeer(i), device_id_type=MESH)
+        pl.when(is_early | is_hub | (target_of(i) >= EARLY))(functools.partial(greet, zpeer(i)))
     for i in range(1, NY):
-        pl.semaphore_signal(barrier, inc=1, device_id=ypeer(i), device_id_type=MESH)
+        greet(ypeer(i))
 
     pairs = (
         (q_h, q_v), (sel_h, sel_s), (len_h, len_s), (xz_h, xz_v), (cs_h, cs_v), (cw_h, cw_v), (cb_h, cb_v),
@@ -90,19 +98,22 @@
     qrow = q_v[0:1, :].astype(F32)
     for k in range(16):
         q_own[k : k + 1, :] = qrow[:, k * HEAD_DIM : (k + 1) * HEAD_DIM]
-    q_all[0] = q_own[...].astype(BF16)
+    q_all[c] = q_own[...].astype(BF16)
 
     loads[1].wait()
     loads[2].wait()
-    shard_id = lax.broadcasted_iota(jnp.int32, (NZ, 128), 0)
-    slot_id = lax.broadcasted_iota(jnp.int32, (NZ, 128), 1)
-    entry = jnp.where(slot_id < POOL, shard_id * POOL + slot_id, -1)
-    count = jnp.zeros((NZ, 128), jnp.int32)
+    lane = lax.broadcasted_iota(jnp.int32, (1, 128), 1)
+    listed = jnp.where(lane == TOPK, len_s[0, 0], -1)
     for k in range(TOPK):
-        amount = len_s[0, 0] if k == 0 else PAGE
-        count = jnp.where(entry == sel_s[0, k], amount, count)
-    cnt_send[:, 0, :] = count.astype(F32)
-    cnt_all[0] = cnt_send[c]
+        listed = jnp.where(lane == k, sel_s[0, k], listed)
+    sel_all[c] = listed
+    z_recv[c] = jnp.zeros((16, 128), BF16)
+    zb_recv[c] = jnp.zeros((1, 128), F32)
+
+    @pl.when(is_rest)
+    def _():
+        z_recv[0:EARLY] = jnp.zeros((EARLY, 16, 128), BF16)
+        zb_recv[0:EARLY] = jnp.zeros((EARLY, 1, 128), F32)
 
     for k in (3, 4, 5, 6):
         loads[k].wait()
@@ -126,33 +137,79 @@
     own_value = jnp.where(half, nkv[:, 128:256], nkv[:, 384:512])
     own_score = jnp.sum(q_own[...] * own_key, axis=1, keepdims=True) * SCALE2
     tokens = POOL * PAGE
-    lane = lax.broadcasted_iota(jnp.int32, (1, 128), 1)
     low_half = lane < PAGE
-    token = jnp.where(low_half, lane, lane - PAGE).astype(F32)
+    token = jnp.where(low_half, lane, lane - PAGE)
+    entry = jnp.where(lane < POOL, c * POOL + lane, -1)
     for k in range(9, 16):
         loads[k].wait()
     gain = jnp.concatenate(
         [jnp.broadcast_to(gain_v[0:1, j * 128 : (j + 1) * 128], (4, 128)) for j in range(4)], axis=0
     )
 
-    pl.semaphore_wait(barrier, NZ - 1 + NY - 1)
+    pl.semaphore_wait(barrier, jnp.where(is_early, EARLY, NZ - 1) + NY - 1)
 
     for i in range(1, NY):
         send(y_send.at[lax.rem(h + i, NY)], y_recv.at[i - 1], y_ss, y_rs, ypeer(i))
-    for i in FAR_FIRST:
-        g = group_of(i)
-        send(q_all.at[0], q_all.at[SLOT_OF[i]], q_ss, q_rs.at[g], zpeer(i))
-        send(cnt_send.at[lax.rem(c + i, NZ)], cnt_all.at[SLOT_OF[i]], c_ss, c_rs.at[g], zpeer(i))
+
+    def drain_rows(n, *pairs):
+        for ref, sem in pairs:
+            drain(ref.at[pl.ds(0, n)], sem)
+
+    def send_query(dev, group):
+        send(q_all.at[c], q_all.at[c], q_ss, q_rs.at[group], dev)
+        send(sel_all.at[c], sel_all.at[c], c_ss, c_rs.at[group], dev)
+
+    @pl.when(is_early)
+    def _():
+        for to in (HUB, *range(EARLY)):
+            pl.when(c != to)(functools.partial(send_query, (r, h, jnp.int32(to)), 0))
+
+    @pl.when(is_hub)
+    def _():
+        drain_rows(EARLY, (q_all, q_rs.at[0]), (sel_all, c_rs.at[0]))
+        block = pl.ds(0, EARLY)
+        for k, to in enumerate(HUB_ORDER):
+            dev = (r, h, jnp.int32(to))
+            send(q_all.at[block], q_all.at[block], f_ss.at[k], q_rs.at[0], dev)
+            send(sel_all.at[block], sel_all.at[block], fc_ss.at[k], c_rs.at[0], dev)
+
+    @pl.when(is_late)
+    def _():
+        for i in FAR_FIRST:
+            send_query(zpeer(i), 1)
 
     total = y_send[h]
     drain(y_recv, y_rs)
     for i in range(NY - 1):
         total = total + y_recv[i]
-    z_send[...] = total[0:16].astype(BF16)
-    zb_send[...] = total[16:17]
-    for i in FAR_FIRST:
-        send(z_send, z_recv.at[i - 1], z_ss, z_rs, zpeer(i))
-        send(zb_send, zb_recv.at[i - 1], zb_ss, zb_rs, zpeer(i))
+    z_send[0] = total[0:16].astype(BF16)
+    zb_send[0] = total[16:17]
+
+    def send_sums(dev, which, group):
+        send(z_send.at[which], z_recv.at[c], z_ss, z_rs.at[group], dev)
+        send(zb_send.at[which], zb_recv.at[c], zb_ss, zb_rs.at[group], dev)
+
+    @pl.when(is_early)
+    def _():
+        for to in (HUB, *range(EARLY)):
+            pl.when(c != to)(functools.partial(send_sums, (r, h, jnp.int32(to)), 0, 0))
+
+    @pl.when(is_hub)
+    def _():
+        drain_rows(EARLY, (z_recv, z_rs.at[0]), (zb_recv, zb_rs.at[0]))
+        z_send[1] = (total[0:16] + jnp.sum(z_recv[0:EARLY].astype(F32), axis=0)).astype(BF16)
+        zb_send[1] = total[16:17] + jnp.sum(zb_recv[0:EARLY], axis=0)
+        for to in range(EARLY):
+            send_sums((r, h, jnp.int32(to)), 0, 1)
+        for to in HUB_ORDER:
+            send_sums((r, h, jnp.int32(to)), 1, 1)
+
+    @pl.when(is_rest)
+    def _():
+        for to in range(EARLY):
+            send_sums((r, h, jnp.int32(to)), 0, 1)
+        for i in FAR_FIRST:
+            pl.when(target_of(i) >= EARLY)(functools.partial(send_sums, zpeer(i), 0, 1))
 
     diagonal = (
         lax.broadcasted_iota(jnp.int32, (1, 16, HEAD_DIM), 1)
@@ -160,9 +217,18 @@
     )
     for g, (first, last) in enumerate(GROUPS):
         n = last - first
-        drain(cnt_all.at[part_of(first, last)], c_rs.at[g])
-        drain(q_all.at[part_of(first, last)], q_rs.at[g])
-        counts = cnt_all[first:last, 0, :]
+        arrivals = (q_all, q_rs.at[g]), (sel_all, c_rs.at[g])
+        if g == 0:
+            pl.when(is_early)(functools.partial(drain_rows, EARLY - 1, *arrivals))
+            pl.when(is_rest)(functools.partial(drain_rows, EARLY, *arrivals))
+        else:
+            pl.when(is_early)(functools.partial(drain_rows, NZ - EARLY, *arrivals))
+            pl.when(is_late)(functools.partial(drain_rows, NZ - EARLY - 1, *arrivals))
+        listed = sel_all[first:last, 0, :]
+        counts = jnp.zeros((n, 128), jnp.int32)
+        for k in range(TOPK):
+            amount = listed[:, TOPK : TOPK + 1] if k == 0 else PAGE
+            counts = jnp.where(listed[:, k : k + 1] == entry, amount, counts)
         bias = jnp.concatenate(
             [
                 jnp.where(
@@ -192,20 +258,23 @@
         level = jnp.concatenate(levels, axis=1)
         p_send[first:last] = jnp.concatenate(outs, axis=1).astype(BF16)
         pl_send[first:last] = jnp.sum(jnp.where(diagonal, level, 0.0), axis=1, keepdims=True)
-        for i in SLOTS[first:last][::-1]:
-            if i:
-                k, back = SLOT_OF[i], NZ - i
-                slot, to = SLOT_OF[back], group_of(back)
-                send(p_send.at[k], p_recv.at[slot], p_ss, p_rs.at[to], zpeer(back))
-                send(pl_send.at[k], pl_recv.at[slot], pl_ss, pl_rs.at[to], zpeer(back))
+
+        def send_part(to):
+            dev = (r, h, jnp.int32(to))
+            send(p_send.at[to], p_recv.at[c], p_ss, p_rs.at[c // HALF], dev)
+            send(pl_send.at[to], pl_recv.at[c], pl_ss, pl_rs.at[c // HALF], dev)
+
+        for to in range(first, last):
+            pl.when(c != to)(functools.partial(send_part, to))
 
     total = total[0:16]
-    terms = zb_send[...]
-    drain(z_recv, z_rs)
-    drain(zb_recv, zb_rs)
-    for i in SLOTS[1:]:
-        total = total + z_recv[i - 1].astype(F32)
-        terms = terms + zb_recv[i - 1]
+    terms = zb_send[0]
+    pl.when(is_early)(functools.partial(drain_rows, EARLY - 1, (z_recv, z_rs.at[0]), (zb_recv, zb_rs.at[0])))
+    others = (z_recv, z_rs.at[1]), (zb_recv, zb_rs.at[1])
+    pl.when(is_early)(functools.partial(drain_rows, NZ - EARLY, *others))
+    pl.when(is_late)(functools.partial(drain_rows, NZ - EARLY - 1, *others))
+    total = total + jnp.sum(z_recv[...].astype(F32), axis=0)
+    terms = terms + jnp.sum(zb_recv[...], axis=0)
     square = total * total
     square = square[0:8] + square[8:16]
     square = square + jnp.concatenate([square[4:8], square[0:4]], axis=0)
@@ -235,12 +304,13 @@
         yout[i : i + 1, :] = jnp.sum(terms[low + 16 : low + 32, k : k + 1] * new, axis=0, keepdims=True)
     mamba_v[...] = ((yout[...] + dskip_v[0:1, :] * mixed) * gate).astype(BF16)
 
-    p_recv[0] = p_send[0]
-    pl_recv[0] = pl_send[0]
+    p_recv[c] = p_send[c]
+    pl_recv[c] = pl_send[c]
     top, weight, summed = own_score, jnp.ones_like(own_score), own_value
-    for g, (first, last) in enumerate(GROUPS):
-        drain(pl_recv.at[part_of(first, last)], pl_rs.at[g])
-        drain(p_recv.at[part_of(first, last)], p_rs.at[g])
+    for g, (first, last) in enumerate(((0, HALF), (HALF, NZ))):
+        arrivals = (pl_recv, pl_rs.at[g]), (p_recv, p_rs.at[g])
+        pl.when(c // HALF == g)(functools.partial(drain_rows, HALF - 1, *arrivals))
+        pl.when(c // HALF != g)(functools.partial(drain_rows, HALF, *arrivals))
         level = jnp.sum(jnp.where(diagonal, pl_recv[first:last], 0.0), axis=2, keepdims=True)
         new_top = jnp.maximum(top, jnp.max(level, axis=0))
         old = jnp.exp2(top - new_top)
@@ -252,12 +322,17 @@
     for k in range(16):
         attn_v[0:1, k * HEAD_DIM : (k + 1) * HEAD_DIM] = joined[k : k + 1, :]
 
-    peers = pl.ds(1, NZ - 1)
-    for ref, sem in (
-        (y_recv, y_ss), (q_all.at[peers], q_ss), (cnt_all.at[peers], c_ss), (z_recv, z_ss), (zb_recv, zb_ss),
-        (y_recv, g_ss), (p_recv.at[peers], p_ss), (pl_recv.at[peers], pl_ss),
-    ):
-        drain(ref, sem)
+    drain(y_recv, y_ss)
+    drain(y_recv, g_ss)
+    drain_rows(NZ - 1, (p_recv, p_ss), (pl_recv, pl_ss))
+    sent = (q_all, q_ss), (sel_all, c_ss), (z_recv, z_ss), (zb_recv, zb_ss)
+    pl.when(is_early)(functools.partial(drain_rows, EARLY, *sent))
+    pl.when(is_late)(functools.partial(drain_rows, NZ - 1, *sent))
+
+    @pl.when(is_hub)
+    def _():
+        for k in range(len(HUB_ORDER)):
+            drain_rows(EARLY, (q_all, f_ss.at[k]), (sel_all, fc_ss.at[k]))
 
 
 def hand_over(a_in, b_in, c_in, a_out, b_out, c_out, sem):
@@ -290,14 +365,13 @@
     scratch += [
         pltpu.VMEM((16, HEAD_DIM), F32),
         pltpu.VMEM((NZ, 16, HEAD_DIM), BF16),
-        pltpu.VMEM((NZ, 1, 128), F32),
-        pltpu.VMEM((NZ, 1, 128), F32),
+        pltpu.VMEM((NZ, 1, 128), jnp.int32),
         pltpu.VMEM((NY, 17, 128), F32),
         pltpu.VMEM((NY - 1, 17, 128), F32),
-        pltpu.VMEM((16, 128), BF16),
-        pltpu.VMEM((1, 128), F32),
-        pltpu.VMEM((NZ - 1, 16, 128), BF16),
-        pltpu.VMEM((NZ - 1, 1, 128), F32),
+        pltpu.VMEM((2, 16, 128), BF16),
+        pltpu.VMEM((2, 1, 128), F32),
+        pltpu.VMEM((NZ, 16, 128), BF16),
+        pltpu.VMEM((NZ, 1, 128), F32),
         pltpu.VMEM((NY, 17, 128), F32),
         pltpu.VMEM((NZ, 16, HEAD_DIM), BF16),
         pltpu.VMEM((NZ, 1, 128), F32),
@@ -306,8 +380,9 @@
         pltpu.VMEM((16, 256), F32),
         pltpu.SemaphoreType.DMA((len(args),)),
     ]
-    one, grouped = pltpu.SemaphoreType.DMA, pltpu.SemaphoreType.DMA((len(GROUPS),))
-    scratch += [one, grouped, one, grouped, one, one, one, one, one, one, one, one, one, grouped, one, grouped]
+    one, two = pltpu.SemaphoreType.DMA, pltpu.SemaphoreType.DMA((2,))
+    scratch += [one, two, one, two] + [pltpu.SemaphoreType.DMA((len(HUB_ORDER),))] * 2
+    scratch += [one, one, one, two, one, two, one, one, one, two, one, two]
     made = pl.pallas_call(
         kernel,
         out_shape=[pltpu.VMEM(*o) for o in outs],

time: 32.9 us -> 32.5 us (0.988)
  Pallas kernels: 31.4 us -> 31 us
    pallas_call x1, Pallas kernels: 30.7 us -> 30.3 us  [on_device(): pl.pallas_call(kernel, out_shape=[pltpu.VMEM(*o) for o in outs], in_specs...]
where the time goes in v4:
time: 32.5 us; the launch traced here: 32.3 us
  Pallas kernels  31 us (95%)
  between operations  1.29 us (4%)
    pallas_call x1, Pallas kernels, on_device(): pl.pallas_call(kernel, out_shape=[pltpu.VMEM(*o) for o in outs], in_specs...  30.3 us
    pallas_call x1, Pallas kernels, on_device(): pl.pallas_call(hand_over, out_shape=[jax.ShapeDtypeStruct(*o) for o in ou...  0.74 us

profile of v4, /device:TPU:6, one launch (start us, length us, event | category | flops | bytes accessed | tf_op | source)
XLA Modules:
  0.0 32.3 jit_solution(3017718642122679128)
XLA Ops:
  1.3 30.3 %decode_step.1 = (bf16[16,256]{1,0:T(8,128)(2,1)S(1)}, f32[16,16,256]{2,1,0:T(8,128)S(1)}, bf16[1,2048]{1,0:T(2,128)(2,1)S(1)}) custom-call(bf16[16,2,256]{2,1,0:T(2,128)(2,1)} %xz_h.1, bf16[3,16,256]{2,1,0:T(8,128)(2,1)} %bitcast.9, f32[16,16,256]{2,1,0:T(8,128)} %ssm_h.1, f32[4,256]{1,0:T(4,128)} %cw_h.1, f32[1,256]{1,0:T(1,128)} %bitcast.11, ...), custom_call_target="tpu_custom_call" | custom-call | tf_op jit(solution)/shard_map/decode_step/pallas_call | solution.py:386
  31.6 0.7 %hand_over.1 = (bf16[16,256]{1,0:T(8,128)(2,1)}, f32[16,16,256]{2,1,0:T(8,128)}, bf16[1,2048]{1,0:T(2,128)(2,1)}) custom-call(bf16[16,256]{1,0:T(8,128)(2,1)S(1)} %get-tuple-element.6.a_in, f32[16,16,256]{2,1,0:T(8,128)S(1)} %get-tuple-element.7.b_in, bf16[1,2048]{1,0:T(2,128)(2,1)S(1)} %get-tuple-element.8.c_in), custom_call_target="tpu_custom_call" | custom-call | tf_op jit(solution)/shard_map/hand_over/pallas_call | solution.py:397

commit v5 on v4

--- a/solution.py
+++ b/solution.py
@@ -27,9 +27,9 @@
 
 FAR_FIRST = (8, 9, 7, 10, 6, 11, 5, 12, 4, 13, 3, 14, 2, 15, 1)
 EARLY = 1
-HUB = 4
-HUB_ORDER = tuple(t for t in (8, 9, 10, 12, 11, 13, 14, 7, 6, 15, 5, 4, 3, 2, 1) if t >= EARLY and t != HUB)
-GROUPS = ((0, EARLY), (EARLY, NZ))
+APART = 4
+FORWARD_ORDER = (8, 9, 10, 12, 11, 13, 14, 7, 6, 15, 5, 4, 3, 2, 1)
+GROUPS = ((0, EARLY), (EARLY, NZ // 2), (NZ // 2, NZ))
 HALF = NZ // 2
 SCALE2 = math.log2(math.e) / math.sqrt(HEAD_DIM)
 NT = (((1,), (1,)), ((), ()))
@@ -69,8 +69,9 @@
 
     is_early = c < EARLY
     is_late = c >= EARLY
-    is_hub = c == HUB
-    is_rest = is_late & (c != HUB)
+    mine = c - APART
+    is_hub = (mine >= 0) & (mine < EARLY)
+    is_rest = is_late & jnp.logical_not(is_hub)
 
     def target_of(i):
         return lax.rem(c + i, NZ)
@@ -81,7 +82,7 @@
         pl.semaphore_signal(barrier, inc=1, device_id=dev, device_id_type=MESH)
 
     for i in FAR_FIRST:
-        pl.when(is_early | is_hub | (target_of(i) >= EARLY))(functools.partial(greet, zpeer(i)))
+        pl.when(is_early | (target_of(i) >= EARLY) | (is_hub & (target_of(i) == mine)))(functools.partial(greet, zpeer(i)))
     for i in range(1, NY):
         greet(ypeer(i))
 
@@ -110,10 +111,12 @@
     z_recv[c] = jnp.zeros((16, 128), BF16)
     zb_recv[c] = jnp.zeros((1, 128), F32)
 
-    @pl.when(is_rest)
-    def _():
-        z_recv[0:EARLY] = jnp.zeros((EARLY, 16, 128), BF16)
-        zb_recv[0:EARLY] = jnp.zeros((EARLY, 1, 128), F32)
+    for e in range(EARLY):
+
+        @pl.when(is_late & (mine != e))
+        def _():
+            z_recv[e] = jnp.zeros((16, 128), BF16)
+            zb_recv[e] = jnp.zeros((1, 128), F32)
 
     for k in (3, 4, 5, 6):
         loads[k].wait()
@@ -159,24 +162,34 @@
         send(q_all.at[c], q_all.at[c], q_ss, q_rs.at[group], dev)
         send(sel_all.at[c], sel_all.at[c], c_ss, c_rs.at[group], dev)
 
+    def each_early(act):
+        for to in range(EARLY):
+            pl.when(c != to)(functools.partial(act, (r, h, jnp.int32(to))))
+
+    def each_late(act):
+        for to in FORWARD_ORDER:
+            if to >= EARLY:
+                pl.when(c != to)(functools.partial(act, (r, h, jnp.int32(to))))
+
     @pl.when(is_early)
     def _():
-        for to in (HUB, *range(EARLY)):
-            pl.when(c != to)(functools.partial(send_query, (r, h, jnp.int32(to)), 0))
+        send_query((r, h, c + APART), 3)
+        each_early(lambda dev: send_query(dev, 0))
 
     @pl.when(is_hub)
     def _():
-        drain_rows(EARLY, (q_all, q_rs.at[0]), (sel_all, c_rs.at[0]))
-        block = pl.ds(0, EARLY)
-        for k, to in enumerate(HUB_ORDER):
-            dev = (r, h, jnp.int32(to))
-            send(q_all.at[block], q_all.at[block], f_ss.at[k], q_rs.at[0], dev)
-            send(sel_all.at[block], sel_all.at[block], fc_ss.at[k], c_rs.at[0], dev)
+        drain_rows(1, (q_all, q_rs.at[3]), (sel_all, c_rs.at[3]))
+
+        def forward(dev):
+            send(q_all.at[mine], q_all.at[mine], f_ss, q_rs.at[0], dev)
+            send(sel_all.at[mine], sel_all.at[mine], fc_ss, c_rs.at[0], dev)
+
+        each_late(forward)
 
     @pl.when(is_late)
     def _():
         for i in FAR_FIRST:
-            send_query(zpeer(i), 1)
+            send_query(zpeer(i), 1 + c // HALF)
 
     total = y_send[h]
     drain(y_recv, y_rs)
@@ -191,18 +204,16 @@
 
     @pl.when(is_early)
     def _():
-        for to in (HUB, *range(EARLY)):
-            pl.when(c != to)(functools.partial(send_sums, (r, h, jnp.int32(to)), 0, 0))
+        send_sums((r, h, c + APART), 0, 2)
+        each_early(lambda dev: send_sums(dev, 0, 0))
 
     @pl.when(is_hub)
     def _():
-        drain_rows(EARLY, (z_recv, z_rs.at[0]), (zb_recv, zb_rs.at[0]))
-        z_send[1] = (total[0:16] + jnp.sum(z_recv[0:EARLY].astype(F32), axis=0)).astype(BF16)
-        zb_send[1] = total[16:17] + jnp.sum(zb_recv[0:EARLY], axis=0)
-        for to in range(EARLY):
-            send_sums((r, h, jnp.int32(to)), 0, 1)
-        for to in HUB_ORDER:
-            send_sums((r, h, jnp.int32(to)), 1, 1)
+        drain_rows(1, (z_recv, z_rs.at[2]), (zb_recv, zb_rs.at[2]))
+        z_send[1] = (total[0:16] + z_recv[mine].astype(F32)).astype(BF16)
+        zb_send[1] = total[16:17] + zb_recv[mine]
+        each_early(lambda dev: send_sums(dev, 0, 1))
+        each_late(lambda dev: send_sums(dev, 1, 1))
 
     @pl.when(is_rest)
     def _():
@@ -211,6 +222,28 @@
         for i in FAR_FIRST:
             pl.when(target_of(i) >= EARLY)(functools.partial(send_sums, zpeer(i), 0, 1))
 
+    own_total = total
+
+    def finish_sums():
+        total = own_total[0:16]
+        terms = zb_send[0]
+        if EARLY > 1:
+            pl.when(is_early)(functools.partial(drain_rows, EARLY - 1, (z_recv, z_rs.at[0]), (zb_recv, zb_rs.at[0])))
+        others = (z_recv, z_rs.at[1]), (zb_recv, zb_rs.at[1])
+        pl.when(is_early)(functools.partial(drain_rows, NZ - EARLY, *others))
+        pl.when(is_late)(functools.partial(drain_rows, NZ - EARLY - 1, *others))
+        total = total + jnp.sum(z_recv[...].astype(F32), axis=0)
+        terms = terms + jnp.sum(zb_recv[...], axis=0)
+        square = total * total
+        square = square[0:8] + square[8:16]
+        square = square + jnp.concatenate([square[4:8], square[0:4]], axis=0)
+        square = jnp.sum(square, axis=1, keepdims=True) * (1.0 / DT_RANK)
+        inv = lax.rsqrt(square + EPS)
+        g_recv[h, 0:16, :] = total * jnp.concatenate([inv, inv], axis=0) * gain
+        g_recv[h, 16:17, :] = terms
+        for i in range(1, NY):
+            send(g_recv.at[h], g_recv.at[h], g_ss, g_rs, ypeer(i))
+
     diagonal = (
         lax.broadcasted_iota(jnp.int32, (1, 16, HEAD_DIM), 1)
         == lax.broadcasted_iota(jnp.int32, (1, 16, HEAD_DIM), 2)
@@ -219,11 +252,15 @@
         n = last - first
         arrivals = (q_all, q_rs.at[g]), (sel_all, c_rs.at[g])
         if g == 0:
-            pl.when(is_early)(functools.partial(drain_rows, EARLY - 1, *arrivals))
             pl.when(is_rest)(functools.partial(drain_rows, EARLY, *arrivals))
+            if EARLY > 1:
+                pl.when(is_early | is_hub)(functools.partial(drain_rows, EARLY - 1, *arrivals))
         else:
-            pl.when(is_early)(functools.partial(drain_rows, NZ - EARLY, *arrivals))
-            pl.when(is_late)(functools.partial(drain_rows, NZ - EARLY - 1, *arrivals))
+            if g == 2:
+                pl.when(is_early)(finish_sums)
+            inside = (c >= first) & (c < last)
+            pl.when(inside)(functools.partial(drain_rows, n - 1, *arrivals))
+            pl.when(jnp.logical_not(inside))(functools.partial(drain_rows, n, *arrivals))
         listed = sel_all[first:last, 0, :]
         counts = jnp.zeros((n, 128), jnp.int32)
         for k in range(TOPK):
@@ -267,23 +304,7 @@
         for to in range(first, last):
             pl.when(c != to)(functools.partial(send_part, to))
 
-    total = total[0:16]
-    terms = zb_send[0]
-    pl.when(is_early)(functools.partial(drain_rows, EARLY - 1, (z_recv, z_rs.at[0]), (zb_recv, zb_rs.at[0])))
-    others = (z_recv, z_rs.at[1]), (zb_recv, zb_rs.at[1])
-    pl.when(is_early)(functools.partial(drain_rows, NZ - EARLY, *others))
-    pl.when(is_late)(functools.partial(drain_rows, NZ - EARLY - 1, *others))
-    total = total + jnp.sum(z_recv[...].astype(F32), axis=0)
-    terms = terms + jnp.sum(zb_recv[...], axis=0)
-    square = total * total
-    square = square[0:8] + square[8:16]
-    square = square + jnp.concatenate([square[4:8], square[0:4]], axis=0)
-    square = jnp.sum(square, axis=1, keepdims=True) * (1.0 / DT_RANK)
-    inv = lax.rsqrt(square + EPS)
-    g_recv[h, 0:16, :] = total * jnp.concatenate([inv, inv], axis=0) * gain
-    g_recv[h, 16:17, :] = terms
-    for i in range(1, NY):
-        send(g_recv.at[h], g_recv.at[h], g_ss, g_rs, ypeer(i))
+    pl.when(is_late)(finish_sums)
     rate = jnp.exp(alog_v[...])
     gate = silu(xz_v[:, 1, :].astype(F32))
     mixed = mixed_bf.astype(F32)
@@ -329,10 +350,7 @@
     pl.when(is_early)(functools.partial(drain_rows, EARLY, *sent))
     pl.when(is_late)(functools.partial(drain_rows, NZ - 1, *sent))
 
-    @pl.when(is_hub)
-    def _():
-        for k in range(len(HUB_ORDER)):
-            drain_rows(EARLY, (q_all, f_ss.at[k]), (sel_all, fc_ss.at[k]))
+    pl.when(is_hub)(functools.partial(drain_rows, NZ - EARLY - 1, (q_all, f_ss), (sel_all, fc_ss)))
 
 
 def hand_over(a_in, b_in, c_in, a_out, b_out, c_out, sem):
@@ -381,8 +399,9 @@
         pltpu.SemaphoreType.DMA((len(args),)),
     ]
     one, two = pltpu.SemaphoreType.DMA, pltpu.SemaphoreType.DMA((2,))
-    scratch += [one, two, one, two] + [pltpu.SemaphoreType.DMA((len(HUB_ORDER),))] * 2
-    scratch += [one, one, one, two, one, two, one, one, one, two, one, two]
+    three = pltpu.SemaphoreType.DMA((3,))
+    four = pltpu.SemaphoreType.DMA((4,))
+    scratch += [one, four, one, four, one, one, one, one, one, three, one, three, one, one, one, two, one, two]
     made = pl.pallas_call(
         kernel,
         out_shape=[pltpu.VMEM(*o) for o in outs],

time: 32.5 us -> 32.3 us (level)
  no operation moved by 1% of the time
where the time goes in v5:
time: 32.3 us; the launch traced here: 32.1 us
  Pallas kernels  30.8 us (95%)
  between operations  1.29 us (4%)
    pallas_call x1, Pallas kernels, on_device(): pl.pallas_call(kernel, out_shape=[pltpu.VMEM(*o) for o in outs], in_specs...  30.1 us
    pallas_call x1, Pallas kernels, on_device(): pl.pallas_call(hand_over, out_shape=[jax.ShapeDtypeStruct(*o) for o in ou...  0.74 us

profile of v5, /device:TPU:6, one launch (start us, length us, event | category | flops | bytes accessed | tf_op | source)
XLA Modules:
  0.0 32.1 jit_solution(10249065363590433666)
XLA Ops:
  1.3 30.1 %decode_step.1 = (bf16[16,256]{1,0:T(8,128)(2,1)S(1)}, f32[16,16,256]{2,1,0:T(8,128)S(1)}, bf16[1,2048]{1,0:T(2,128)(2,1)S(1)}) custom-call(bf16[16,2,256]{2,1,0:T(2,128)(2,1)} %xz_h.1, bf16[3,16,256]{2,1,0:T(8,128)(2,1)} %bitcast.9, f32[16,16,256]{2,1,0:T(8,128)} %ssm_h.1, f32[4,256]{1,0:T(4,128)} %cw_h.1, f32[1,256]{1,0:T(1,128)} %bitcast.11, ...), custom_call_target="tpu_custom_call" | custom-call | tf_op jit(solution)/shard_map/decode_step/pallas_call | solution.py:405
  31.4 0.7 %hand_over.1 = (bf16[16,256]{1,0:T(8,128)(2,1)}, f32[16,16,256]{2,1,0:T(8,128)}, bf16[1,2048]{1,0:T(2,128)(2,1)}) custom-call(bf16[16,256]{1,0:T(8,128)(2,1)S(1)} %get-tuple-element.6.a_in, f32[16,16,256]{2,1,0:T(8,128)S(1)} %get-tuple-element.7.b_in, bf16[1,2048]{1,0:T(2,128)(2,1)S(1)} %get-tuple-element.8.c_in), custom_call_target="tpu_custom_call" | custom-call | tf_op jit(solution)/shard_map/hand_over/pallas_call | solution.py:416

commit v6 on v5

--- a/solution.py
+++ b/solution.py
@@ -29,7 +29,7 @@
 EARLY = 1
 APART = 4
 FORWARD_ORDER = (8, 9, 10, 12, 11, 13, 14, 7, 6, 15, 5, 4, 3, 2, 1)
-GROUPS = ((0, EARLY), (EARLY, NZ // 2), (NZ // 2, NZ))
+GROUPS = ((0, EARLY), (EARLY, 4), (4, NZ // 2), (NZ // 2, NZ))
 HALF = NZ // 2
 SCALE2 = math.log2(math.e) / math.sqrt(HEAD_DIM)
 NT = (((1,), (1,)), ((), ()))
@@ -159,8 +159,8 @@
             drain(ref.at[pl.ds(0, n)], sem)
 
     def send_query(dev, group):
+        send(sel_all.at[c], sel_all.at[c], c_ss, c_rs.at[group], dev)
         send(q_all.at[c], q_all.at[c], q_ss, q_rs.at[group], dev)
-        send(sel_all.at[c], sel_all.at[c], c_ss, c_rs.at[group], dev)
 
     def each_early(act):
         for to in range(EARLY):
@@ -173,12 +173,12 @@
 
     @pl.when(is_early)
     def _():
-        send_query((r, h, c + APART), 3)
+        send_query((r, h, c + APART), 4)
         each_early(lambda dev: send_query(dev, 0))
 
     @pl.when(is_hub)
     def _():
-        drain_rows(1, (q_all, q_rs.at[3]), (sel_all, c_rs.at[3]))
+        drain_rows(1, (q_all, q_rs.at[4]), (sel_all, c_rs.at[4]))
 
         def forward(dev):
             send(q_all.at[mine], q_all.at[mine], f_ss, q_rs.at[0], dev)
@@ -189,7 +189,7 @@
     @pl.when(is_late)
     def _():
         for i in FAR_FIRST:
-            send_query(zpeer(i), 1 + c // HALF)
+            send_query(zpeer(i), jnp.where(c < 4, 1, 2 + c // HALF))
 
     total = y_send[h]
     drain(y_recv, y_rs)
@@ -219,8 +219,8 @@
     def _():
         for to in range(EARLY):
             send_sums((r, h, jnp.int32(to)), 0, 1)
-        for i in FAR_FIRST:
-            pl.when(target_of(i) >= EARLY)(functools.partial(send_sums, zpeer(i), 0, 1))
+        for to in range(EARLY, NZ):
+            pl.when(c != to)(functools.partial(send_sums, (r, h, jnp.int32(to)), 0, 1))
 
     own_total = total
 
@@ -256,7 +256,7 @@
             if EARLY > 1:
                 pl.when(is_early | is_hub)(functools.partial(drain_rows, EARLY - 1, *arrivals))
         else:
-            if g == 2:
+            if g == 3:
                 pl.when(is_early)(finish_sums)
             inside = (c >= first) & (c < last)
             pl.when(inside)(functools.partial(drain_rows, n - 1, *arrivals))
@@ -400,7 +400,7 @@
     ]
     one, two = pltpu.SemaphoreType.DMA, pltpu.SemaphoreType.DMA((2,))
     three = pltpu.SemaphoreType.DMA((3,))
-    four = pltpu.SemaphoreType.DMA((4,))
+    four = pltpu.SemaphoreType.DMA((5,))
     scratch += [one, four, one, four, one, one, one, one, one, three, one, three, one, one, one, two, one, two]
     made = pl.pallas_call(
         kernel,

time: 32.3 us -> 32.3 us (level)
  no operation moved by 1% of the time
where the time goes in v6:
time: 32.3 us; the launch traced here: 32.1 us
  Pallas kernels  30.8 us (95%)
  between operations  1.29 us (4%)
    pallas_call x1, Pallas kernels, on_device(): pl.pallas_call(kernel, out_shape=[pltpu.VMEM(*o) for o in outs], in_specs...  30.1 us
    pallas_call x1, Pallas kernels, on_device(): pl.pallas_call(hand_over, out_shape=[jax.ShapeDtypeStruct(*o) for o in ou...  0.74 us

profile of v6, /device:TPU:6, one launch (start us, length us, event | category | flops | bytes accessed | tf_op | source)
XLA Modules:
  0.0 32.1 jit_solution(10611699415334399900)
XLA Ops:
  1.3 30.1 %decode_step.1 = (bf16[16,256]{1,0:T(8,128)(2,1)S(1)}, f32[16,16,256]{2,1,0:T(8,128)S(1)}, bf16[1,2048]{1,0:T(2,128)(2,1)S(1)}) custom-call(bf16[16,2,256]{2,1,0:T(2,128)(2,1)} %xz_h.1, bf16[3,16,256]{2,1,0:T(8,128)(2,1)} %bitcast.9, f32[16,16,256]{2,1,0:T(8,128)} %ssm_h.1, f32[4,256]{1,0:T(4,128)} %cw_h.1, f32[1,256]{1,0:T(1,128)} %bitcast.11, ...), custom_call_target="tpu_custom_call" | custom-call | tf_op jit(solution)/shard_map/decode_step/pallas_call | solution.py:405
  31.4 0.7 %hand_over.1 = (bf16[16,256]{1,0:T(8,128)(2,1)}, f32[16,16,256]{2,1,0:T(8,128)}, bf16[1,2048]{1,0:T(2,128)(2,1)}) custom-call(bf16[16,256]{1,0:T(8,128)(2,1)S(1)} %get-tuple-element.6.a_in, f32[16,16,256]{2,1,0:T(8,128)S(1)} %get-tuple-element.7.b_in, bf16[1,2048]{1,0:T(2,128)(2,1)S(1)} %get-tuple-element.8.c_in), custom_call_target="tpu_custom_call" | custom-call | tf_op jit(solution)/shard_map/hand_over/pallas_call | solution.py:416
